TPU v7x, 256 devices: a whole 4x4x8 slice. The times are simulated.
256 devices in a mesh: gx: 4 (over y_hi, core), yz: 64 (over x, z, y_lo).
Axes of the slice: x: 4, y: 4 (y_hi: 2, y_lo: 2; y = y_hi * 2 + y_lo), z: 8, core: 2. Of those that a mesh axis runs over, the one named last changes fastest.
Arguments:
- prefill_tokens: bfloat16 [512, 18432], P('gx'), may hold values from -6 to 6
- prefill_lengths: int32 [4], P('gx'), may hold values from 1 to 128, as said below
- decode_tokens: bfloat16 [2, 256, 18432], P(None, None, ('gx', 'yz')), may hold values from -6 to 6
- cache_lengths: int32 [256], P(('gx', 'yz')), may hold values from 1 to 2048, as said below
- cache_keyvals: bfloat16 [256, 2048, 512], P(('gx', 'yz')), may hold values from -6 to 6
- query_weight: bfloat16 [18432, 12288], P('gx', 'yz')
- keyval_weight: bfloat16 [18432, 512], P('gx', 'yz')
- out_weight: bfloat16 [12288, 18432], P('yz', 'gx'), may hold values from -0.0546875 to 0.0546875
Outputs:
- prefill_out: bfloat16 [512, 18432], P('gx', 'yz')
- decode_out: bfloat16 [2, 256, 18432], P(None, None, ('gx', 'yz'))
Inputs may be any that keep to these rules, and one draw needn't show every extreme that they name: `prefill_lengths`: some prefill sequence has exactly 128 valid positions. `cache_lengths`: some decode row has exactly 2048 valid cached positions.
All inputs are finite; a program needn't handle non-finite values.
Results may differ from a plain program's by a relative error of at most 0.015.
Values may be sent and summed in bfloat16 or wider, within the bound.
A program may use at most 128 MiB of HBM per device.

v0:
```python
import jax
import jax.numpy as jnp
from jax import lax
from jax.sharding import PartitionSpec as P

HEADS = 48
HD = 256
PLEN = 128


def project_inputs(rows_input, query_weight, keyval_weight):
    portion = lax.all_gather(rows_input, "yz", axis=1, tiled=True)
    query_sum = jnp.dot(portion, query_weight, preferred_element_type=jnp.float32)
    keyval_sum = jnp.dot(portion, keyval_weight, preferred_element_type=jnp.float32)
    query_part, keyval_part = (
        lax.psum_scatter(query_sum, "gx", scatter_dimension=0, tiled=True),
        lax.psum_scatter(keyval_sum, "gx", scatter_dimension=0, tiled=True),
    )
    return (
        lax.all_to_all(
            query_part.astype(jnp.bfloat16), "yz", split_axis=0, concat_axis=1, tiled=True
        ),
        lax.all_to_all(
            keyval_part.astype(jnp.bfloat16), "yz", split_axis=0, concat_axis=1, tiled=True
        ),
    )


def project_outputs(attended_rows, out_weight):
    returned = lax.all_to_all(attended_rows, "yz", split_axis=1, concat_axis=0, tiled=True)
    partial_terms = jnp.dot(
        lax.all_gather(returned, "gx", axis=0, tiled=True),
        out_weight,
        preferred_element_type=jnp.float32,
    )
    return lax.psum_scatter(partial_terms, "yz", scatter_dimension=1, tiled=True)


def attend_cache(row_queries, new_keyvals, cache_keys, cache_values, visible):
    score_scale = HD ** (-0.5)
    cache_scores = (
        jnp.einsum("rhd,rld->rhl", row_queries, cache_keys, preferred_element_type=jnp.float32)
        * score_scale
    )
    cache_scores = jnp.where(visible[:, None, :], cache_scores, -1e30)
    fresh_scores = (
        jnp.einsum(
            "rhd,rnd->rhn", row_queries, new_keyvals[..., :HD], preferred_element_type=jnp.float32
        )
        * score_scale
    )
    peak_score = jnp.maximum(
        jnp.max(cache_scores, axis=-1, keepdims=True), jnp.max(fresh_scores, axis=-1, keepdims=True)
    )
    cache_exp = jnp.exp(cache_scores - peak_score)
    fresh_exp = jnp.exp(fresh_scores - peak_score)
    denominator = jnp.sum(cache_exp, axis=-1, keepdims=True) + jnp.sum(
        fresh_exp, axis=-1, keepdims=True
    )
    cache_probs = (cache_exp / denominator).astype(jnp.bfloat16)
    fresh_probs = (fresh_exp / denominator).astype(jnp.bfloat16)
    attended = jnp.einsum(
        "rhl,rld->rhd", cache_probs, cache_values, preferred_element_type=jnp.float32
    )
    attended = attended + jnp.einsum(
        "rhn,rnd->rhd", fresh_probs, new_keyvals[..., HD:], preferred_element_type=jnp.float32
    )
    return attended.astype(jnp.bfloat16).reshape(row_queries.shape[0], HEADS * HD)


def body(
    prefill_tokens,
    prefill_lengths,
    decode_tokens,
    cache_lengths,
    cache_keyvals,
    query_weight,
    keyval_weight,
    out_weight,
):
    token_count = prefill_tokens.shape[0]
    query_sum = jnp.dot(
        prefill_tokens,
        lax.all_gather(query_weight, "gx", axis=0, tiled=True),
        preferred_element_type=jnp.float32,
    )
    keyval_sum = jnp.dot(
        prefill_tokens,
        lax.all_gather(keyval_weight, "gx", axis=0, tiled=True),
        preferred_element_type=jnp.float32,
    )
    query_local = query_sum.astype(jnp.bfloat16)
    keyval_local = keyval_sum.astype(jnp.bfloat16)
    keyval_all = lax.all_gather(keyval_local, "yz", axis=1, tiled=True)
    query_rows = lax.all_to_all(query_local, "yz", split_axis=0, concat_axis=1, tiled=True)
    query_count = query_rows.shape[0]
    query_pos = lax.axis_index("yz") * query_count + jnp.arange(query_count, dtype=jnp.int32)
    key_pos = jnp.arange(token_count, dtype=jnp.int32)
    query_seq = query_pos // PLEN
    key_seq = key_pos // PLEN
    seq_ids = jnp.arange(prefill_lengths.shape[0], dtype=jnp.int32)
    query_len = jnp.sum(
        jnp.where(query_seq[:, None] == seq_ids[None, :], prefill_lengths[None, :], 0), axis=1
    )
    allowed = (query_seq[:, None] == key_seq[None, :]) & (key_pos[None, :] <= query_pos[:, None])
    allowed = allowed & ((key_pos % PLEN)[None, :] < query_len[:, None])
    queries = query_rows.reshape(query_count, HEADS, HD)
    scores = jnp.einsum(
        "qhd,kd->qhk", queries, keyval_all[:, :HD], preferred_element_type=jnp.float32
    ) * HD ** (-0.5)
    scores = jnp.where(allowed[:, None, :], scores, -1e30)
    peak_score = jnp.max(scores, axis=-1, keepdims=True)
    exponent = jnp.exp(scores - peak_score)
    pre_probs = (exponent / jnp.sum(exponent, axis=-1, keepdims=True)).astype(jnp.bfloat16)
    attended = jnp.einsum(
        "qhk,kd->qhd", pre_probs, keyval_all[:, HD:], preferred_element_type=jnp.float32
    )
    attended = attended.astype(jnp.bfloat16).reshape(query_count, HEADS * HD)
    returned = lax.all_to_all(attended, "yz", split_axis=1, concat_axis=0, tiled=True)
    partial_terms = jnp.dot(
        returned,
        lax.all_gather(out_weight, "gx", axis=1, tiled=True),
        preferred_element_type=jnp.float32,
    )
    prefill_out = lax.psum_scatter(partial_terms, "yz", scatter_dimension=1, tiled=True).astype(
        jnp.bfloat16
    )
    cache_keys = cache_keyvals[:, :, :HD]
    cache_values = cache_keyvals[:, :, HD:]
    owned_rows = cache_keyvals.shape[0]
    visible = jnp.arange(cache_keyvals.shape[1], dtype=jnp.int32)[None, :] < cache_lengths[:, None]
    step_count = decode_tokens.shape[0]
    fresh_list = []
    step_outputs = []
    for step_index in range(step_count):
        step_query, step_keyval = project_inputs(
            decode_tokens[step_index], query_weight, keyval_weight
        )
        fresh_list.append(step_keyval)
        new_keyvals = jnp.stack(fresh_list, axis=1)
        attended_rows = attend_cache(
            step_query.reshape(owned_rows, HEADS, HD),
            new_keyvals,
            cache_keys,
            cache_values,
            visible,
        )
        step_outputs.append(project_outputs(attended_rows, out_weight))
    decode_out = jnp.stack(step_outputs, axis=0).astype(jnp.bfloat16)
    return (prefill_out, decode_out)


def solution(mesh):
    in_specs = (
        P("gx", None),
        P("gx"),
        P(None, None, ("gx", "yz")),
        P(("gx", "yz")),
        P(("gx", "yz"), None, None),
        P("gx", "yz"),
        P("gx", "yz"),
        P("yz", "gx"),
    )
    out_specs = (P("gx", "yz"), P(None, None, ("gx", "yz")))
    return jax.shard_map(body, mesh=mesh, in_specs=in_specs, out_specs=out_specs, check_vma=False)
```

profile of v0, /device:TPU:16, one launch (start us, length us, event | category | flops | bytes accessed | tf_op | source)
XLA Modules:
  0.0 1857.1 jit_solution(14454317168121392903)
XLA Ops:
  9.5 304.9 %all-gather.15.cloned.1.call-done = bf16[1,256,4608]{1,2,0:T(8,128)(2,1)} async-done(((bf16[1,256,72]{1,2,0:T(8,128)(2,1)}), bf16[1,256,4608]{1,2,0:T(8,128)(2,1)}) %all-gather.15.cloned.1.call-update) | async-done | bytes 2359312 | tf_op jit(solution)/shard_map/all_gather | solution.py:12
  317.6 297.7 %all-gather.13.cloned.1.call-done = bf16[1,256,4608]{1,2,0:T(8,128)(2,1)} async-done(((bf16[1,256,72]{1,2,0:T(8,128)(2,1)}), bf16[1,256,4608]{1,2,0:T(8,128)(2,1)}) %all-gather.13.cloned.1.call-update) | async-done | bytes 2359312 | tf_op jit(solution)/shard_map/all_gather | solution.py:12
  626.5 18.3 reduce-scatter.24.cloned.1.call-done
  646.3 11.7 all-to-all-start.6
  658.7 19.9 %reduce-scatter.22.cloned.1.call-done = f32[64,8]{1,0:T(8,128)} async-done(((f32[256,8]{1,0:T(8,128)}), f32[64,8]{1,0:T(8,128)}) %reduce-scatter.22.cloned.1.call-update) | async-done | bytes 2064
  680.2 11.7 all-to-all-start.3
  691.9 20.6 %reduce-scatter.18.cloned.1.call-done = f32[64,192]{1,0:T(8,128)} async-done(((f32[256,192]{1,0:T(8,128)}), f32[64,192]{1,0:T(8,128)}) %reduce-scatter.18.cloned.1.call-update) | async-done | bytes 49168 | tf_op jit(solution)/shard_map/reduce_scatter | solution.py:16
  714.0 11.9 all-to-all-start.5
  726.4 10.0 all-to-all-done.5
  740.9 14.4 all_to_all.121
  755.3 6.9 all-gather.3
  767.1 4.6 all-to-all-start.2
  772.0 10.3 all-to-all-done.2
  786.4 14.4 all_to_all.122
  800.8 6.9 all-gather.1
  811.6 7.5 all_gather.25
  822.9 8.3 convolution_convert_fusion.1
  831.9 4.6 all-to-all-start
  836.7 157.2 %all_gather.26 = bf16[128,512]{0,1:T(8,128)(2,1)S(1)} all-gather(bf16[128,8]{0,1:T(8,128)(2,1)S(1)} %convolution_convert_fusion.2), channel_id=1, replica_groups=mesh['gx'=4,'yz'=64] {'yz'}, dimensions={1}, use_global_device_ids=true | all-gather | bytes 133120 | tf_op jit(solution)/shard_map/all_gather | solution.py:94
  994.8 14.3 all_to_all.123
  1009.2 10.4 fusion.56
  1019.7 176.4 %reduce-scatter.20.cloned.1.call-done = f32[256,72]{0,1:T(8,128)} async-done(((f32[256,4608]{0,1:T(8,128)}), f32[256,72]{0,1:T(8,128)}) %reduce-scatter.20.cloned.1.call-update) | async-done | bytes 73744 | tf_op jit(solution)/shard_map/reduce_scatter | solution.py:36
  1197.0 319.3 %reduce-scatter.16.cloned.1.call-done = f32[256,72]{0,1:T(8,128)} async-done(((f32[256,4608]{0,1:T(8,128)}), f32[256,72]{0,1:T(8,128)}) %reduce-scatter.16.cloned.1.call-update) | async-done | bytes 73744 | tf_op jit(solution)/shard_map/reduce_scatter | solution.py:36
  1517.8 331.2 %reduce-scatter.12.cloned.1.call-done = f32[128,288]{0,1:T(8,128)} async-done(((f32[128,18432]{0,1:T(8,128)}), f32[128,288]{0,1:T(8,128)}) %reduce-scatter.12.cloned.1.call-update) | async-done | bytes 147472 | tf_op jit(solution)/shard_map/reduce_scatter | solution.py:125
  (95 shorter events, 48.2 us)
Async XLA Ops:
  7.2 608.1 %copy-start.2 = (bf16[4608,8]{0,1:T(8,128)(2,1)S(1)}, bf16[4608,8]{0,1:T(8,128)(2,1)}, u32[]{:S(2)}) copy-start(bf16[4608,8]{0,1:T(8,128)(2,1)} %param.14) | copy-start | bytes 221188
  7.2 307.2 %all-gather.15.cloned.1.call-start = ((), (), s32[]{:S(2)}) async-start(), calls=%async_computation.23 | async-start | bytes 2396160 | tf_op jit(solution)/shard_map/all_gather | solution.py:12
  8.7 606.6 %all-gather.13.cloned.1.call-start = ((), (), s32[]{:S(2)}) async-start(), calls=%async_computation.22 | async-start | bytes 2396160 | tf_op jit(solution)/shard_map/all_gather | solution.py:12
  9.4 609.1 %copy-start.1 = (bf16[4608,192]{0,1:T(8,128)(2,1)S(1)}, bf16[4608,192]{0,1:T(8,128)(2,1)}, u32[]{:S(2)}) copy-start(bf16[4608,192]{0,1:T(8,128)(2,1)} %param.13) | copy-start | bytes 5308420
  9.4 635.3 %reduce-scatter.24.cloned.1.call-start = ((), (), s32[]{:S(2)}) async-start(), calls=%async_computation.25 | async-start | bytes 163840
  317.5 361.1 %reduce-scatter.22.cloned.1.call-start = ((), (), s32[]{:S(2)}) async-start(), calls=%async_computation.24 | async-start | bytes 163840
  618.5 94.0 %reduce-scatter.18.cloned.1.call-start = ((), (), s32[]{:S(2)}) async-start(), calls=%async_computation.20 | async-start | bytes 327680 | tf_op jit(solution)/shard_map/reduce_scatter | solution.py:16
  621.7 143.9 %reduce-scatter.14.cloned.1.call-start = ((), (), s32[]{:S(2)}) async-start(), calls=%async_computation.18 | async-start | bytes 327680 | tf_op jit(solution)/shard_map/reduce_scatter | solution.py:16
  625.0 197.9 %all-gather.9.cloned.1.call-start = ((), (), s32[]{:S(2)}) async-start(), calls=%async_computation.15 | async-start | bytes 8847360 | tf_op jit(solution)/shard_map/all_gather | solution.py:84
  625.7 383.4 %all-gather.11.cloned.1.call-start = ((), (), s32[]{:S(2)}) async-start(), calls=%async_computation.16 | async-start | bytes 8847360 | tf_op jit(solution)/shard_map/all_gather | solution.py:122
  646.3 33.8 %all-to-all-start.6 = ((bf16[64,1,8]{2,1,0:T(2,128)(2,1)}), bf16[64,1,8]{2,1,0:T(2,128)(2,1)S(1)}, u32[]{:S(2)}, u32[]{:S(2)}) async-start(bf16[64,1,8]{2,1,0:T(2,128)(2,1)} %copy.55), calls=%async_computation.10 | async-start | bytes 65536 | tf_op jit(solution)/shard_map/all_to_all | solution.py:23
  680.2 33.9 %all-to-all-start.3 = ((bf16[64,1,8]{2,1,0:T(2,128)(2,1)}), bf16[64,1,8]{2,1,0:T(2,128)(2,1)S(1)}, u32[]{:S(2)}, u32[]{:S(2)}) async-start(bf16[64,1,8]{2,1,0:T(2,128)(2,1)} %copy.50), calls=%async_computation.5 | async-start | bytes 65536 | tf_op jit(solution)/shard_map/all_to_all | solution.py:23
  714.0 22.4 %all-to-all-start.5 = ((bf16[64,1,192]{2,1,0:T(2,128)(2,1)}), bf16[64,1,192]{2,1,0:T(2,128)(2,1)S(1)}, u32[]{:S(2)}, u32[]{:S(2)}) async-start(bf16[64,1,192]{2,1,0:T(2,128)(2,1)} %copy.54), calls=%async_computation.9 | async-start | bytes 131072 | tf_op jit(solution)/shard_map/all_to_all | solution.py:20
  726.0 470.1 %reduce-scatter.20.cloned.1.call-start = ((), (), s32[]{:S(2)}) async-start(), calls=%async_computation.21 | async-start | bytes 4792320 | tf_op jit(solution)/shard_map/reduce_scatter | solution.py:36
  736.8 25.4 %copy-start = (bf16[192,4608]{1,0:T(8,128)(2,1)S(1)}, bf16[192,4608]{1,0:T(8,128)(2,1)}, u32[]{:S(2)}) copy-start(bf16[192,4608]{1,0:T(8,128)(2,1)} %param.15) | copy-start | bytes 5308420
  767.1 15.1 all-to-all-start.2
  771.7 744.5 %reduce-scatter.16.cloned.1.call-start = ((), (), s32[]{:S(2)}) async-start(), calls=%async_computation.19 | async-start | bytes 4792320 | tf_op jit(solution)/shard_map/reduce_scatter | solution.py:36
  831.9 161.9 %all-to-all-start = ((bf16[64,2,192]{2,1,0:T(2,128)(2,1)}), bf16[64,2,192]{2,1,0:T(2,128)(2,1)S(1)}, u32[]{:S(2)}, u32[]{:S(2)}) async-start(bf16[64,2,192]{2,1,0:T(2,128)(2,1)} %all_to_all.90), calls=%async_computation | async-start | bytes 131072 | tf_op jit(solution)/shard_map/all_to_all | solution.py:95
  836.6 1012.4 %reduce-scatter.12.cloned.1.call-start = ((), (), s32[]{:S(2)}) async-start(), calls=%async_computation.17 | async-start | bytes 9584640 | tf_op jit(solution)/shard_map/reduce_scatter | solution.py:125
Sparse Core Ops, SparseCore 0:
  10.4 303.9 all-gather.14
  316.7 298.5 all-gather.12
  618.0 26.7 reduce-scatter.23
  647.5 31.0 reduce-scatter.21
  681.2 31.2 reduce-scatter.17
  715.3 31.5 reduce-scatter.13
  748.7 58.6 all-gather.8
  809.2 58.4 all-gather.10
  870.2 325.8 reduce-scatter.19
  1198.4 317.7 reduce-scatter.15
  1518.8 330.1 reduce-scatter.11
where the time goes:
time: 1860 us
  waiting for transfers between devices  1510 us (81%)
  blocking collectives  222 us (12%)
  matrix products  49.3 us (3%)
  starting transfers between devices  45.2 us (2%)
    all_gather x2, waiting for transfers between devices, project_inputs(): portion = lax.all_gather(rows_input, 'yz', axis=1, tiled=True)  603 us
    reduce_scatter x2, waiting for transfers between devices, project_outputs(): lax.psum_scatter(partial_terms, 'yz', scatter_dimension=1, tiled=True)  496 us
    reduce_scatter x1, waiting for transfers between devices, body(): lax.psum_scatter(partial_terms, 'yz', scatter_dimension=1, tiled=True)  331 us
    all_gather x1, blocking collectives, body(): keyval_all = lax.all_gather(keyval_local, 'yz', axis=1, tiled=True)  157 us
    unnamed x13, waiting for transfers between devices  40.4 us
  transfers between devices with their start and end apart: 16, of which 10 were waited for; matrix products, arithmetic and copies ran while one was open for 3% of the time, Pallas kernels for 0%

commit v1 on v0

v1 whole, which is shorter than its diff:
```python
import functools
import heapq

import jax
import jax.numpy as jnp
from jax import lax
from jax.experimental import pallas as pl
from jax.experimental.pallas import tpu as pltpu
from jax.sharding import PartitionSpec as P

HEADS = 48
HD = 256
PLEN = 128
GX, X, Z, YL = 4, 4, 8, 2
BLK = 144
TOK = 1024
WIDTH = {"a": 640, "b": 384}
COLS = 192
KVC = 8
ROWS1 = 208
MESH = pl.DeviceIdType.MESH
F32 = jnp.float32
BF16 = jnp.bfloat16
FULL, UPPER, LOWER = (0, 144), (0, 80), (80, 64)


def steps_from(key):
    kind, xo, zo = key
    out = []
    if kind == "a":
        if xo == 0:
            if -3 < zo <= 0:
                out.append(("z+", FULL, ("a", 0, zo - 1)))
            if zo == -3:
                out.append(("z+", UPPER, ("a", 0, 4)))
            if 0 <= zo < 3:
                out.append(("z-", FULL, ("a", 0, zo + 1)))
            if zo == 3:
                out.append(("z-", LOWER, ("a", 0, 4)))
            out.append(("x+", FULL, ("a", -1, zo)))
            out.append(("x-", FULL, ("a", 1, zo)))
        elif xo == -1 and zo % 2 == 0:
            out.append(("x+", FULL, ("a", 2, zo)))
        elif xo == 1 and zo % 2 == 1:
            out.append(("x-", FULL, ("a", 2, zo)))
    else:
        if zo == 0:
            if xo == 0:
                out.append(("x+", FULL, ("b", -1, 0)))
                out.append(("x-", FULL, ("b", 1, 0)))
            elif xo == -1:
                out.append(("x+", UPPER, ("b", 2, 0)))
            elif xo == 1:
                out.append(("x-", LOWER, ("b", 2, 0)))
        if zo <= 0 and (zo > -3 or xo in (0, 2)):
            out.append(("z+", FULL, ("b", xo, zo - 1 if zo > -3 else 4)))
        if 0 <= zo <= 3 and (zo < 3 or xo in (-1, 1)):
            out.append(("z-", FULL, ("b", xo, zo + 1)))
    return out


def make_plan():
    free = {d: 0.0 for d in ("x+", "x-", "z+", "z-")}
    events, order, missing, pieces = [], [], {}, {}
    count = 0

    def leave(key, now):
        nonlocal count
        order.append(key)
        for d, rows, there in steps_from(key):
            free[d] = max(free[d], now) + WIDTH[key[0]] * rows[1] / 147456.0 * 2.95
            count += 1
            heapq.heappush(events, (free[d] + 1.0, count, there, (d, rows)))

    order_own = [("b", 0, 0), ("a", 0, 0)]
    for key in order_own:
        leave(key, 0.0)
    while events:
        now, _, key, piece = heapq.heappop(events)
        pieces.setdefault(key, []).append(piece)
        got = sum(p[1][1] for p in pieces[key])
        if got == BLK:
            leave(key, now)
    assert len(order) == 64
    return order, pieces


ORDER, PIECES = make_plan()
OPPOSITE = {"x+": "x-", "x-": "x+", "z+": "z-", "z-": "z+"}
SENDS = {}
for _key in ORDER:
    for _n, _step in enumerate(steps_from(_key)):
        SENDS[(_key, _n)] = len(SENDS)
NSEND = len(SENDS)
FILLS = {}
for _key in ORDER:
    for _n, (_d, _rows, _there) in enumerate(steps_from(_key)):
        FILLS[(_there, _rows)] = SENDS[(_key, _n)]
SLOTS = {k: [key for key in ORDER for _ in steps_from(key) if key[0] == k] for k in "ab"}


def place():
    gx = lax.axis_index("gx")
    yz = lax.axis_index("yz")
    return gx, yz // (Z * YL), (yz // YL) % Z, yz % YL


def device_at(gx, x, z, yl, d):
    dx = {"x+": 1, "x-": X - 1}.get(d, 0)
    dz = {"z+": 1, "z-": Z - 1}.get(d, 0)
    return (gx, ((x + dx) % X) * (Z * YL) + ((z + dz) % Z) * YL + yl)


def greet(gx, x, z, yl):
    barrier = pltpu.get_barrier_semaphore()
    yz = lax.axis_index("yz")
    for d in ("x+", "x-", "z+", "z-"):
        pl.semaphore_signal(barrier, inc=1, device_id=device_at(gx, x, z, yl, d), device_id_type=MESH)
    for g in range(1, GX):
        pl.semaphore_signal(barrier, inc=1, device_id=((gx + g) % GX, yz), device_id_type=MESH)
    pl.semaphore_wait(barrier, 4 + GX - 1)


def project_kernel(xa, xb, wq, wkv, out, ga, gb, w, acc, give, take, send, recv, rsend, rrecv):
    gx, x, z, yl = place()
    yz = lax.axis_index("yz")
    own = {"a": xa, "b": xb}
    held = {"a": ga, "b": gb}

    def slot(key, rows):
        kind, xo, zo = key
        first = pl.multiple_of(((z + zo) % Z) * BLK + rows[0], 16)
        return held[kind].at[(x + xo) % X, pl.ds(first, rows[1])]

    def copy(key, n):
        d, rows, there = steps_from(key)[n]
        k = SENDS[(key, n)]
        src = own[key[0]] if key[1:] == (0, 0) else slot(key, rows)
        return pltpu.make_async_remote_copy(
            src_ref=src,
            dst_ref=slot(key, rows),
            send_sem=send.at[k],
            recv_sem=recv.at[k],
            device_id=device_at(gx, x, z, yl, d),
            device_id_type=MESH,
        )

    def arrived(key):
        for _, rows in PIECES[key]:
            k = FILLS[(key, rows)]
            pltpu.make_async_remote_copy(
                src_ref=slot(key, rows),
                dst_ref=slot(key, rows),
                send_sem=send.at[k],
                recv_sem=recv.at[k],
                device_id=device_at(gx, x, z, yl, "x+"),
                device_id_type=MESH,
            ).wait_recv()

    greet(gx, x, z, yl)
    copies = []
    seen = {}

    def multiply(kind, xo):
        xx = (x + xo) % X
        lanes = slice(0, WIDTH["a"]) if kind == "a" else slice(WIDTH["a"], TOK)
        part = lax.dot_general(
            w[pl.ds(pl.multiple_of(xx * (Z * BLK), 128), Z * BLK), :],
            held[kind][xx],
            (((0,), (0,)), ((), ())),
            preferred_element_type=F32,
        )
        if (kind, "first") in seen:
            acc[:, lanes] += part
        else:
            acc[:, lanes] = part
            seen[(kind, "first")] = True

    for key in ORDER:
        kind, xo, zo = key
        if (xo, zo) != (0, 0):
            arrived(key)
        for n in range(len(steps_from(key))):
            c = copy(key, n)
            c.start()
            copies.append(c)
        if (xo, zo) == (0, 0):
            first = pl.multiple_of(z * BLK, 16)
            held[kind][x, pl.ds(first, BLK), :] = own[kind][...]
        if key == ("a", 0, 0):
            w[:, :COLS] = wq[...]
            w[:, COLS:] = jnp.zeros((wq.shape[0], 256 - COLS), BF16)
            w[:, COLS : COLS + KVC] = wkv[...]
        seen[(kind, xo)] = seen.get((kind, xo), 0) + 1
        if seen[(kind, xo)] == Z:
            multiply(kind, xo)

    for g in range(GX):
        give[g, :, :128] = acc[:ROWS1, g * 128 : g * 128 + 128].astype(give.dtype)
        give[g, :, 128:] = acc[:ROWS1, 512 + g * 128 : 640 + g * 128].astype(give.dtype)
    sums = []
    for s in range(1, GX):
        to = (gx + s) % GX
        c = pltpu.make_async_remote_copy(
            src_ref=give.at[to],
            dst_ref=take.at[s],
            send_sem=rsend.at[s],
            recv_sem=rrecv.at[s],
            device_id=(to, yz),
            device_id_type=MESH,
        )
        c.start()
        sums.append(c)
    for c in copies:
        c.wait_send()
    for c in sums:
        c.wait()
    total = give[gx].astype(F32)
    for s in range(1, GX):
        total = total + take[s].astype(F32)
    out[...] = total.astype(BF16)


def project(xa, xb, wq, wkv):
    depth = wq.shape[0]
    vmem = pl.BlockSpec(memory_space=pltpu.VMEM)
    return pl.pallas_call(
        project_kernel,
        out_shape=jax.ShapeDtypeStruct((ROWS1, 256), BF16),
        in_specs=[vmem] * 4,
        out_specs=vmem,
        scratch_shapes=[
            pltpu.VMEM((X, Z * BLK, WIDTH["a"]), BF16),
            pltpu.VMEM((X, Z * BLK, WIDTH["b"]), BF16),
            pltpu.VMEM((depth, 256), BF16),
            pltpu.VMEM((256, TOK), F32),
            pltpu.VMEM((GX, ROWS1, 256), F32),
            pltpu.VMEM((GX, ROWS1, 256), F32),
            pltpu.SemaphoreType.DMA((NSEND,)),
            pltpu.SemaphoreType.DMA((NSEND,)),
            pltpu.SemaphoreType.DMA((GX,)),
            pltpu.SemaphoreType.DMA((GX,)),
        ],
        compiler_params=pltpu.CompilerParams(
            collective_id=0, has_side_effects=True, vmem_limit_bytes=40 * 2**20
        ),
        name="gather_project",
    )(xa, xb, wq, wkv)


def output_kernel(att, wt, out_a, out_b, heads, dec, pa, pb, ra, rb, send, recv, hsend, hrecv):
    gx, x, z, yl = place()
    yz = lax.axis_index("yz")
    held = {"a": pa, "b": pb}
    landing = {"a": ra, "b": rb}
    where = {}
    used = {"a": 0, "b": 0}
    for key in ORDER:
        for n in range(len(steps_from(key))):
            where[(key, n)] = used[key[0]]
            used[key[0]] += 1

    greet(gx, x, z, yl)
    shares = []
    for s in range(1, GX):
        c = pltpu.make_async_remote_copy(
            src_ref=att,
            dst_ref=heads.at[s],
            send_sem=hsend.at[s],
            recv_sem=hrecv.at[s],
            device_id=((gx + s) % GX, yz),
            device_id_type=MESH,
        )
        c.start()
        shares.append(c)
    heads[0] = att[...]
    for c in shares:
        c.wait()
    for s in range(GX):
        lane = pl.multiple_of(((gx - s + GX) % GX) * 128, 128)
        dec[:, pl.ds(lane, 128)] = heads[s, :, :128]

    def terms(key):
        kind, xo, zo = key
        xx, zz = (x + xo) % X, (z + zo) % Z
        group = heads[(gx - xx + GX) % GX, :, 128:]

        def prefill(q):
            first = pl.multiple_of(zz * (4 * BLK) + q * BLK, 16)
            return jnp.dot(wt[pl.ds(first, BLK), :], group, preferred_element_type=F32)

        if kind == "a":
            first = pl.multiple_of((xx * Z + zz) * BLK, 16)
            return [
                (0, 512, jnp.dot(wt[pl.ds(first, BLK), :], dec[...], preferred_element_type=F32)),
                (512, 128, prefill(0)),
            ]
        return [(128 * q - 128, 128, prefill(q)) for q in (1, 2, 3)]

    copies = []
    for key in reversed(ORDER):
        kind, xo, zo = key
        last = (xo, zo) == (0, 0)
        xx, zz = (x + xo) % X, (z + zo) % Z
        local = terms(key)
        steps = steps_from(key)
        for n, (d, rows, there) in enumerate(steps):
            k = SENDS[(key, n)]
            spot = landing[kind].at[where[(key, n)], pl.ds(rows[0], rows[1])]
            pltpu.make_async_remote_copy(
                src_ref=spot,
                dst_ref=spot,
                send_sem=send.at[k],
                recv_sem=recv.at[k],
                device_id=device_at(gx, x, z, yl, d),
                device_id_type=MESH,
            ).wait_recv()
        for lane, width, value in local:
            pieces = [value[:80], value[80:]]
            for n, (d, rows, there) in enumerate(steps):
                for i, (r0, rn) in enumerate((UPPER, LOWER)):
                    if rows[0] <= r0 and r0 + rn <= rows[0] + rows[1]:
                        got = landing[kind][where[(key, n)], r0 : r0 + rn, lane : lane + width]
                        pieces[i] = pieces[i] + got.astype(F32)
            for i, (r0, rn) in enumerate((UPPER, LOWER)):
                if last:
                    target = {"a": out_a, "b": out_b}[kind]
                    target[r0 : r0 + rn, lane : lane + width] = pieces[i]
                else:
                    held[kind][xx * Z + zz, r0 : r0 + rn, lane : lane + width] = pieces[i].astype(BF16)
        if not last:
            for d, rows in PIECES[key]:
                k = FILLS[(key, rows)]
                source = [kn for kn, kk in SENDS.items() if kk == k][0]
                c = pltpu.make_async_remote_copy(
                    src_ref=held[kind].at[xx * Z + zz, pl.ds(rows[0], rows[1])],
                    dst_ref=landing[kind].at[where[source], pl.ds(rows[0], rows[1])],
                    send_sem=send.at[k],
                    recv_sem=recv.at[k],
                    device_id=device_at(gx, x, z, yl, OPPOSITE[d]),
                    device_id_type=MESH,
                )
                c.start()
                copies.append(c)
    for c in copies:
        c.wait_send()


def project_out(att, wt):
    vmem = pl.BlockSpec(memory_space=pltpu.VMEM)
    return pl.pallas_call(
        output_kernel,
        out_shape=(
            jax.ShapeDtypeStruct((BLK, WIDTH["a"]), F32),
            jax.ShapeDtypeStruct((BLK, WIDTH["b"]), F32),
        ),
        in_specs=[vmem] * 2,
        out_specs=(vmem, vmem),
        scratch_shapes=[
            pltpu.VMEM((GX, COLS, 256), BF16),
            pltpu.VMEM((COLS, 512), BF16),
            pltpu.VMEM((X * Z, BLK, WIDTH["a"]), BF16),
            pltpu.VMEM((X * Z, BLK, WIDTH["b"]), BF16),
            pltpu.VMEM((len(SLOTS["a"]), BLK, WIDTH["a"]), BF16),
            pltpu.VMEM((len(SLOTS["b"]), BLK, WIDTH["b"]), BF16),
            pltpu.SemaphoreType.DMA((NSEND,)),
            pltpu.SemaphoreType.DMA((NSEND,)),
            pltpu.SemaphoreType.DMA((GX,)),
            pltpu.SemaphoreType.DMA((GX,)),
        ],
        compiler_params=pltpu.CompilerParams(
            collective_id=1, has_side_effects=True, vmem_limit_bytes=48 * 2**20
        ),
        name="output_scatter",
    )(att, wt)


def attention_kernel(info, qd, fresh, cache, qp, kvt, od, op):
    scale = HD ** (-0.5)
    nt = (((1,), (1,)), ((), ()))
    length, prefill_length, first = info[0], info[1], info[2]
    q = qd[...]
    s = lax.dot_general(q, cache[:, :HD], nt, preferred_element_type=F32) * scale
    pos = lax.broadcasted_iota(jnp.int32, s.shape, 1)
    s = jnp.where(pos < length, s, -1e30)
    f = lax.dot_general(q, fresh[:, :HD], nt, preferred_element_type=F32) * scale
    step = lax.broadcasted_iota(jnp.int32, f.shape, 0) // HEADS
    new = lax.broadcasted_iota(jnp.int32, f.shape, 1)
    f = jnp.where(new <= step, f, -1e30)
    peak = jnp.maximum(jnp.max(s, axis=1, keepdims=True), jnp.max(f, axis=1, keepdims=True))
    es, ef = jnp.exp(s - peak), jnp.exp(f - peak)
    total = jnp.sum(es, axis=1, keepdims=True) + jnp.sum(ef, axis=1, keepdims=True)
    attended = jnp.dot((es / total).astype(BF16), cache[:, HD:], preferred_element_type=F32)
    attended += jnp.dot((ef / total).astype(BF16), fresh[:, HD:], preferred_element_type=F32)
    od[...] = attended.astype(BF16)

    s = jnp.dot(qp[...], kvt[:HD, :], preferred_element_type=F32) * scale
    query = first + lax.broadcasted_iota(jnp.int32, s.shape, 0) // HEADS
    pos = lax.broadcasted_iota(jnp.int32, s.shape, 1)
    s = jnp.where((pos <= query) & (pos < prefill_length), s, -1e30)
    e = jnp.exp(s - jnp.max(s, axis=1, keepdims=True))
    p = (e / jnp.sum(e, axis=1, keepdims=True)).astype(BF16)
    op[...] = lax.dot_general(p, kvt[HD:, :], nt, preferred_element_type=F32).astype(BF16)


def attend(info, qd, fresh, cache, qp, kvt):
    vmem = pl.BlockSpec(memory_space=pltpu.VMEM)
    shape = jax.ShapeDtypeStruct(qd.shape, BF16)
    return pl.pallas_call(
        attention_kernel,
        out_shape=(shape, shape),
        in_specs=[pl.BlockSpec(memory_space=pltpu.SMEM)] + [vmem] * 5,
        out_specs=(vmem, vmem),
        compiler_params=pltpu.CompilerParams(vmem_limit_bytes=32 * 2**20),
        name="attend",
    )(info, qd, fresh, cache, qp, kvt)


def body(
    prefill_tokens,
    prefill_lengths,
    decode_tokens,
    cache_lengths,
    cache_keyvals,
    query_weight,
    keyval_weight,
    out_weight,
):
    gx, x, z, yl = place()
    yz = lax.axis_index("yz")
    group = query_weight.shape[0]
    slices = [
        lax.dynamic_slice(prefill_tokens, (0, g * group + (x * Z + z) * BLK), (PLEN, BLK)).T
        for g in range(GX)
    ]
    pre = lax.all_to_all(jnp.stack(slices), "gx", split_axis=0, concat_axis=0, tiled=True)
    pre = pre.transpose(1, 0, 2).reshape(BLK, GX * PLEN)
    dec = decode_tokens.reshape(2, GX, 64, 72).transpose(3, 1, 0, 2).reshape(72, 512)
    other = lax.ppermute(dec, "yz", [(i, i ^ 1) for i in range(X * Z * YL)])
    dec = jnp.where(
        yl == 0, jnp.concatenate([dec, other], axis=0), jnp.concatenate([other, dec], axis=0)
    )
    xa = jnp.concatenate([dec, pre[:, : WIDTH["a"] - 512]], axis=1)
    xb = pre[:, WIDTH["a"] - 512 :]
    qkv = project(xa, xb, query_weight, keyval_weight)

    q = qkv[:COLS].T
    dq = q[:128].reshape(2, 64, COLS).transpose(1, 0, 2).reshape(64, 2 * COLS)
    pq = q[128:].reshape(64, 2 * COLS)
    kv = qkv[COLS : COLS + KVC]
    dkv = kv[:, :128].reshape(KVC, 2, 64).transpose(2, 1, 0).reshape(64, 2 * KVC)
    pkv = jnp.broadcast_to(kv[:, 128:].reshape(1, KVC * PLEN), (64, KVC * PLEN))
    pad = jnp.zeros((64, 112), BF16)
    sent = jnp.concatenate([pkv, dq, pq, dkv, pad], axis=1)
    got = lax.all_to_all(sent, "yz", split_axis=0, concat_axis=0, tiled=True)
    kvt = got[:, :1024].reshape(64 * KVC, PLEN)
    dq = got[:, 1024:1408].reshape(64, 2, COLS).transpose(1, 0, 2).reshape(2 * HEADS, HD)
    pq = got[:, 1408:1792].reshape(64, 2, COLS).transpose(1, 0, 2).reshape(2 * HEADS, HD)
    fresh = got[:, 1792:1808].reshape(64, 2, KVC).transpose(1, 0, 2).reshape(2, 64 * KVC)
    fresh = jnp.pad(fresh, ((0, 126), (0, 0)))
    info = jnp.stack([cache_lengths[0], prefill_lengths[0], yz * 2]).astype(jnp.int32)
    ad, ap = attend(info, dq, fresh, cache_keyvals[0], pq, kvt)

    ad = ad.reshape(2, 64, COLS).transpose(1, 0, 2).reshape(64, 2 * COLS)
    ap = ap.reshape(2, 64, COLS).transpose(1, 0, 2).reshape(64, 2 * COLS)
    got = lax.all_to_all(
        jnp.concatenate([ad, ap], axis=1), "yz", split_axis=0, concat_axis=0, tiled=True
    )
    ad = got[:, : 2 * COLS].reshape(64, 2, COLS).transpose(2, 1, 0).reshape(COLS, 128)
    ap = got[:, 2 * COLS :].reshape(PLEN, COLS).T
    out_a, out_b = project_out(jnp.concatenate([ad, ap], axis=1), out_weight.T)

    pre = jnp.concatenate([out_a[:, 512:], out_b], axis=1)
    dec = out_a[:, :512]
    swap = [(i, i ^ 1) for i in range(X * Z * YL)]
    dec_other = lax.ppermute(jnp.where(yl == 0, dec[72:], dec[:72]), "yz", swap)
    pre_other = lax.ppermute(jnp.where(yl == 0, pre[:, 256:], pre[:, :256]), "yz", swap)
    dec = jnp.where(yl == 0, dec[:72], dec[72:]) + dec_other
    pre = jnp.where(yl == 0, pre[:, :256], pre[:, 256:]) + pre_other
    decode_out = dec.reshape(72, GX, 2, 64).transpose(2, 1, 3, 0).reshape(2, 256, 72)
    turn = []
    for g in range(GX):
        for i in range(X * Z * YL):
            turn.append((g * 64 + i, (i // 16) * 64 + g * 16 + i % 16))
    pre = lax.ppermute(pre.astype(BF16), ("gx", "yz"), turn)
    prefill_out = pre.reshape(BLK, 2, PLEN).transpose(2, 1, 0).reshape(PLEN, 2 * BLK)
    return (prefill_out, decode_out.astype(BF16))


def solution(mesh):
    in_specs = (
        P("gx", None),
        P("gx"),
        P(None, None, ("gx", "yz")),
        P(("gx", "yz")),
        P(("gx", "yz"), None, None),
        P("gx", "yz"),
        P("gx", "yz"),
        P("yz", "gx"),
    )
    out_specs = (P("gx", "yz"), P(None, None, ("gx", "yz")))
    return jax.shard_map(body, mesh=mesh, in_specs=in_specs, out_specs=out_specs, check_vma=False)
```

time: 1860 us -> 222 us (0.12)
  waiting for transfers between devices: 1510 us -> 25.9 us
  blocking collectives: 222 us -> 0 us
  Pallas kernels: 0 us -> 139 us
  matrix products: 49.3 us -> 0 us
    reduce_scatter x5 -> x0, waiting for transfers between devices: 848 us -> none  [the longest x2 496 us: project_outputs(): lax.psum_scatter(partial_terms, 'yz', scatter_dimension=1, tiled=True)]
    all_gather x4 -> x0, waiting for transfers between devices: 603 us -> none  [the longest x2 603 us: project_inputs(): portion = lax.all_gather(rows_input, 'yz', axis=1, tiled=True)]
    all_gather x4 -> x0, blocking collectives: 179 us -> none  [the longest x1 157 us: body(): keyval_all = lax.all_gather(keyval_local, 'yz', axis=1, tiled=True)]
    pallas_call x0 -> x3, Pallas kernels: none -> 139 us  [the longest x1 72.1 us: project(): pl.pallas_call(project_kernel, out_shape=jax.ShapeDtypeStruct((ROWS1, 256...]
    all_to_all x3 -> x0, blocking collectives: 43.1 us -> none  [the longest x2 28.7 us: project_outputs(): lax.all_to_all(attended_rows, 'yz', split_axis=1, concat_axis=0, tiled=True)]
    dot_general x16 -> x0, matrix products: 43 us -> none  [the longest x1 10.4 us: body(): jnp.dot(returned, lax.all_gather(out_weight, 'gx', axis=1, tiled=True), p...]
    unnamed x13 -> x0, waiting for transfers between devices: 40.4 us -> none
    all_to_all x5 -> x3, starting transfers between devices: 44.5 us -> 19.3 us  [the longest x1 7.6 us: body(): lax.all_to_all(jnp.concatenate([ad, ap], axis=1), 'yz', split_axis=0, con...]
  transfers between devices with their start and end apart: 16 -> 7, of which waited for: 10 -> 4; matrix products, arithmetic and copies ran while one was open for 3% -> 5% of each run, Pallas kernels for 0% -> 0%
where the time goes in v1:
time: 222 us; the launch traced here: 220 us
  Pallas kernels  139 us (63%)
  starting transfers between devices  28.8 us (13%)
  waiting for transfers between devices  25.9 us (12%)
  local copies, waits for them, and re-layouts  19.1 us (9%)
  other arithmetic  4.92 us (2%)
  between operations  2.38 us (1%)
    pallas_call x1, Pallas kernels, project(): pl.pallas_call(project_kernel, out_shape=jax.ShapeDtypeStruct((ROWS1, 256...  72.1 us
    pallas_call x1, Pallas kernels, project_out(): pl.pallas_call(output_kernel, out_shape=(jax.ShapeDtypeStruct((BLK, WIDTH...  65.3 us
    all_to_all x1, waiting for transfers between devices, body(): got = lax.all_to_all(sent, 'yz', split_axis=0, concat_axis=0, tiled=True)  10.3 us
    unnamed x14, local copies, waits for them, and re-layouts  9.33 us
    all_to_all x1, waiting for transfers between devices, body(): lax.all_to_all(jnp.concatenate([ad, ap], axis=1), 'yz', split_axis=0, con...  7.87 us
    all_to_all x1, starting transfers between devices, body(): lax.all_to_all(jnp.concatenate([ad, ap], axis=1), 'yz', split_axis=0, con...  7.6 us
    all_to_all x1, starting transfers between devices, body(): got = lax.all_to_all(sent, 'yz', split_axis=0, concat_axis=0, tiled=True)  6.88 us
    ppermute x1, starting transfers between devices, body(): pre = lax.ppermute(pre.astype(BF16), ('gx', 'yz'), turn)  6 us
  transfers between devices with their start and end apart: 7, of which 4 were waited for; matrix products, arithmetic and copies ran while one was open for 5% of the time, Pallas kernels for 0%

profile of v1, /device:TPU:16, one launch (start us, length us, event | category | flops | bytes accessed | tf_op | source)
XLA Modules:
  0.0 220.3 jit_solution(10159506060377634582)
XLA Ops:
  0.6 1.0 reshape.86
  2.6 1.3 collective-permute-start
  3.8 1.2 constant_dynamic-slice_fusion.3
  6.2 4.8 %all-to-all-start = ((bf16[4,144,128]{2,1,0:T(8,128)(2,1)}), bf16[4,144,128]{2,1,0:T(8,128)(2,1)}, u32[]{:S(2)}, u32[]{:S(2)}) async-start(bf16[4,144,128]{2,1,0:T(8,128)(2,1)} %pad_maximum_fusion.2), calls=%async_computation | async-start | bytes 294912 | tf_op jit(solution)/shard_map/all_to_all | solution.py:436
  11.0 2.7 %copy.97.wq = bf16[4608,192]{1,0:T(8,128)(2,1)S(1)} copy(bf16[4608,192]{0,1:T(8,128)(2,1)} %param.13) | data formatting | bytes 3538944 | tf_op args[5]
  13.7 1.4 copy.98.wkv
  15.1 1.7 maximum_select_fusion
  16.8 0.9 copy_bitcast_fusion
  17.8 0.9 pad_maximum_fusion.xa
  18.7 72.1 %gather_project.1 = bf16[208,256]{1,0:T(8,128)(2,1)S(1)} custom-call(bf16[144,640]{1,0:T(8,128)(2,1)S(1)} %pad_maximum_fusion.xa, bf16[144,384]{1,0:T(8,128)(2,1)S(1)} %slice.83.xb, bf16[4608,192]{1,0:T(8,128)(2,1)S(1)} %copy.97.wq, bf16[4608,8]{1,0:T(8,128)(2,1)S(1)} %copy.98.wkv), custom_call_target="tpu_custom_call" | custom-call | tf_op jit(solution)/shard_map/gather_project/pallas_call | solution.py:227
  92.9 1.0 reshape.110
  93.9 6.9 %all-to-all-start.1 = ((bf16[64,2,960]{2,1,0:T(2,128)(2,1)}), bf16[64,2,960]{2,1,0:T(2,128)(2,1)S(1)}, u32[]{:S(2)}, u32[]{:S(2)}) async-start(bf16[64,2,960]{2,1,0:T(2,128)(2,1)} %reshape.110), calls=%async_computation.1 | async-start | bytes 524288 | tf_op jit(solution)/shard_map/all_to_all | solution.py:455
  102.2 10.3 %all-to-all-done.1 = bf16[64,2,960]{2,1,0:T(2,128)(2,1)S(1)} async-done(((bf16[64,2,960]{2,1,0:T(2,128)(2,1)}), bf16[64,2,960]{2,1,0:T(2,128)(2,1)S(1)}, u32[]{:S(2)}, u32[]{:S(2)}) %all-to-all-start.1) | async-done | bytes 245792 | tf_op jit(solution)/shard_map/all_to_all | solution.py:455
  112.9 0.9 copy.105
  114.7 1.8 attend.1
  118.4 7.6 %all-to-all-start.2 = ((bf16[64,2,384]{2,1,0:T(2,128)(2,1)}), bf16[64,2,384]{2,1,0:T(2,128)(2,1)S(1)}, u32[]{:S(2)}, u32[]{:S(2)}) async-start(bf16[64,2,384]{2,1,0:T(2,128)(2,1)} %reshape.112), calls=%async_computation.2 | async-start | bytes 196608 | tf_op jit(solution)/shard_map/all_to_all | solution.py:466
  126.0 2.7 %copy.116 = bf16[192,4608]{0,1:T(8,128)(2,1)S(1)} copy(bf16[192,4608]{1,0:T(8,128)(2,1)} %param.15) | data formatting | bytes 3538944 | tf_op args[7]
  128.7 7.9 %all-to-all-done.2 = bf16[64,2,384]{2,1,0:T(2,128)(2,1)S(1)} async-done(((bf16[64,2,384]{2,1,0:T(2,128)(2,1)}), bf16[64,2,384]{2,1,0:T(2,128)(2,1)S(1)}, u32[]{:S(2)}, u32[]{:S(2)}) %all-to-all-start.2) | async-done | bytes 98336 | tf_op jit(solution)/shard_map/all_to_all | solution.py:466
  137.2 65.3 %output_scatter.1 = (f32[144,640]{1,0:T(8,128)S(1)}, f32[144,384]{1,0:T(8,128)S(1)}) custom-call(bf16[192,256]{1,0:T(8,128)(2,1)S(1)} %pad_maximum_fusion.3.att, bf16[4608,192]{1,0:T(8,128)(2,1)S(1)} %bitcast.65), custom_call_target="tpu_custom_call" | custom-call | tf_op jit(solution)/shard_map/output_scatter/pallas_call | solution.py:351
  202.6 0.9 collective-permute-start.1
  203.5 1.3 collective-permute-start.3
  204.8 4.6 %collective-permute-done.1 = f32[144,256]{1,0:T(8,128)S(1)} collective-permute-done((f32[144,256]{1,0:T(8,128)S(1)}, f32[144,256]{1,0:T(8,128)S(1)}, u32[]{:S(2)}, u32[]{:S(2)}) %collective-permute-start.1) | collective-permute-done | bytes 147488 | tf_op jit(solution)/shard_map/ppermute | solution.py:477
  209.5 6.0 %collective-permute-start.2 = (bf16[144,256]{1,0:T(8,128)(2,1)S(1)}, bf16[144,256]{1,0:T(8,128)(2,1)S(1)}, u32[]{:S(2)}, u32[]{:S(2)}) collective-permute-start(bf16[144,256]{1,0:T(8,128)(2,1)S(1)} %add_convert_fusion.1), channel_id=1, source_target_pairs={{0,0},{1,1},{2,2},{3,3},{4,4},{5,5},{6,6},{7,7},{8,8},{9,9},{10,10... | collective-permute-start | bytes 221192 | tf_op jit(solution)/shard_map/ppermute | solution.py:485
  216.5 3.1 %collective-permute-done.2 = bf16[144,256]{1,0:T(8,128)(2,1)S(1)} collective-permute-done((bf16[144,256]{1,0:T(8,128)(2,1)S(1)}, bf16[144,256]{1,0:T(8,128)(2,1)S(1)}, u32[]{:S(2)}, u32[]{:S(2)}) %collective-permute-start.2) | collective-permute-done | bytes 73760 | tf_op jit(solution)/shard_map/ppermute | solution.py:485
  (72 shorter events, 9.7 us)
Async XLA Ops:
  2.6 12.5 %collective-permute-start = (bf16[72,512]{1,0:T(8,128)(2,1)}, bf16[72,512]{1,0:T(8,128)(2,1)}, u32[]{:S(2)}, u32[]{:S(2)}) collective-permute-start(bf16[72,512]{1,0:T(8,128)(2,1)} %reshape.87), channel_id=1, source_target_pairs={{0,1},{1,0},{2,3},{3,2},{4,5},{5,4},{6,7},{7,6},{8,9},{9,8},{10,11... | collective-permute-start | bytes 221192 | tf_op jit(solution)/shard_map/ppermute | solution.py:439
  6.2 10.6 %all-to-all-start = ((bf16[4,144,128]{2,1,0:T(8,128)(2,1)}), bf16[4,144,128]{2,1,0:T(8,128)(2,1)}, u32[]{:S(2)}, u32[]{:S(2)}) async-start(bf16[4,144,128]{2,1,0:T(8,128)(2,1)} %pad_maximum_fusion.2), calls=%async_computation | async-start | bytes 294912 | tf_op jit(solution)/shard_map/all_to_all | solution.py:436
  93.9 20.8 %copy-start = (bf16[1,2048,512]{2,1,0:T(8,128)(2,1)S(1)}, bf16[1,2048,512]{2,1,0:T(8,128)(2,1)}, u32[]{:S(2)}) copy-start(bf16[1,2048,512]{2,1,0:T(8,128)(2,1)} %param.12) | copy-start | bytes 6291460
  93.9 18.6 %all-to-all-start.1 = ((bf16[64,2,960]{2,1,0:T(2,128)(2,1)}), bf16[64,2,960]{2,1,0:T(2,128)(2,1)S(1)}, u32[]{:S(2)}, u32[]{:S(2)}) async-start(bf16[64,2,960]{2,1,0:T(2,128)(2,1)} %reshape.110), calls=%async_computation.1 | async-start | bytes 524288 | tf_op jit(solution)/shard_map/all_to_all | solution.py:455
  118.4 18.2 %all-to-all-start.2 = ((bf16[64,2,384]{2,1,0:T(2,128)(2,1)}), bf16[64,2,384]{2,1,0:T(2,128)(2,1)S(1)}, u32[]{:S(2)}, u32[]{:S(2)}) async-start(bf16[64,2,384]{2,1,0:T(2,128)(2,1)} %reshape.112), calls=%async_computation.2 | async-start | bytes 196608 | tf_op jit(solution)/shard_map/all_to_all | solution.py:466
  202.6 6.8 %collective-permute-start.1 = (f32[144,256]{1,0:T(8,128)S(1)}, f32[144,256]{1,0:T(8,128)S(1)}, u32[]{:S(2)}, u32[]{:S(2)}) collective-permute-start(f32[144,256]{1,0:T(8,128)S(1)} %slice_select_fusion.1), channel_id=1, source_target_pairs={{0,1},{1,0},{2,3},{3,2},{4,5},{5,4},{6,7},{7,6},{8,9},{9,8},{10,11... | collective-permute-start | bytes 442376 | tf_op jit(solution)/shard_map/ppermute | solution.py:477
  203.5 12.0 %collective-permute-start.3 = (f32[72,512]{1,0:T(8,128)S(1)}, f32[72,512]{1,0:T(8,128)S(1)}, u32[]{:S(2)}, u32[]{:S(2)}) collective-permute-start(f32[72,512]{1,0:T(8,128)S(1)} %slice_select_fusion), channel_id=1, source_target_pairs={{0,1},{1,0},{2,3},{3,2},{4,5},{5,4},{6,7},{7,6},{8,9},{9,8},{10,11... | collective-permute-start | bytes 442376 | tf_op jit(solution)/shard_map/ppermute | solution.py:476
  209.5 10.2 %collective-permute-start.2 = (bf16[144,256]{1,0:T(8,128)(2,1)S(1)}, bf16[144,256]{1,0:T(8,128)(2,1)S(1)}, u32[]{:S(2)}, u32[]{:S(2)}) collective-permute-start(bf16[144,256]{1,0:T(8,128)(2,1)S(1)} %add_convert_fusion.1), channel_id=1, source_target_pairs={{0,0},{1,1},{2,2},{3,3},{4,4},{5,5},{6,6},{7,7},{8,8},{9,9},{10,10... | collective-permute-start | bytes 221192 | tf_op jit(solution)/shard_map/ppermute | solution.py:485

commit v2 on v0

v2 whole, which is shorter than its diff:
```python
import heapq

import jax
import jax.numpy as jnp
from jax import lax
from jax.experimental import pallas as pl
from jax.experimental.pallas import tpu as pltpu
from jax.sharding import PartitionSpec as P

HEADS = 48
HD = 256
PLEN = 128
GX, X, Z, YL = 4, 4, 8, 2
BLK = 144
TOK = 512
WIDTH = {"pa": 256, "pb": 256, "da": 384, "db": 128}
START = {"pa": 0, "pb": 256, "da": 0, "db": 384}
KINDS = tuple(WIDTH)
COLS = 192
KVC = 8
ROWS1 = 208
MESH = pl.DeviceIdType.MESH
F32 = jnp.float32
BF16 = jnp.bfloat16
FULL, UPPER, LOWER = (0, 144), (0, 80), (80, 64)
OPPOSITE = {"x+": "x-", "x-": "x+", "z+": "z-", "z-": "z+"}


def steps_from(key):
    kind, xo, zo = key
    out = []
    if kind[1] == "a":
        if xo == 0:
            if -3 < zo <= 0:
                out.append(("z+", FULL, (kind, 0, zo - 1)))
            if zo == -3:
                out.append(("z+", UPPER, (kind, 0, 4)))
            if 0 <= zo < 3:
                out.append(("z-", FULL, (kind, 0, zo + 1)))
            if zo == 3:
                out.append(("z-", LOWER, (kind, 0, 4)))
            out.append(("x+", FULL, (kind, -1, zo)))
            out.append(("x-", FULL, (kind, 1, zo)))
        elif xo == -1 and zo % 2 == 0:
            out.append(("x+", FULL, (kind, 2, zo)))
        elif xo == 1 and zo % 2 == 1:
            out.append(("x-", FULL, (kind, 2, zo)))
    else:
        if zo == 0:
            if xo == 0:
                out.append(("x+", FULL, (kind, -1, 0)))
                out.append(("x-", FULL, (kind, 1, 0)))
            elif xo == -1:
                out.append(("x+", UPPER, (kind, 2, 0)))
            elif xo == 1:
                out.append(("x-", LOWER, (kind, 2, 0)))
        if zo <= 0 and (zo > -3 or xo in (0, 2)):
            out.append(("z+", FULL, (kind, xo, zo - 1 if zo > -3 else 4)))
        if 0 <= zo <= 3 and (zo < 3 or xo in (-1, 1)):
            out.append(("z-", FULL, (kind, xo, zo + 1)))
    return out


class Plan:
    def __init__(self, kinds):
        free = dict.fromkeys(OPPOSITE, 0.0)
        events, self.order, self.times, self.pieces = [], [], {}, {}
        self.sends, self.fills, self.source, self.where = {}, {}, {}, {}
        self.slots = dict.fromkeys(kinds, 0)

        def leave(key, now):
            self.order.append(key)
            self.times[key] = now
            for n, (d, rows, there) in enumerate(steps_from(key)):
                free[d] = max(free[d], now) + WIDTH[key[0]] * rows[1] * 4e-5
                k = len(self.sends)
                self.sends[(key, n)] = k
                self.fills[(there, rows)] = k
                self.source[k] = (key, n)
                self.where[(key, n)] = self.slots[key[0]]
                self.slots[key[0]] += 1
                heapq.heappush(events, (free[d] + 1.0, k, there, (d, rows)))

        for kind in kinds:
            leave((kind, 0, 0), 0.0)
        while events:
            now, _, key, piece = heapq.heappop(events)
            self.pieces.setdefault(key, []).append(piece)
            if sum(p[1][1] for p in self.pieces[key]) == BLK:
                leave(key, now)
        assert len(self.order) == X * Z * len(kinds)
        self.end = max(self.times.values())


IN = Plan(("pb", "pa", "db", "da"))
OUT = Plan(("db", "da", "pb", "pa"))
NSEND = len(IN.sends)


def place():
    gx = lax.axis_index("gx")
    yz = lax.axis_index("yz")
    return gx, yz // (Z * YL), (yz // YL) % Z, yz % YL


def flat(x, z, yl):
    return x * (Z * YL) + z * YL + yl


def copy_rows(move):
    def four(g, carry):
        for j in range(4):
            move(g // 4, (g % 4) * 2 + j // 2, j % 2, g, j)
        return carry

    lax.fori_loop(0, 16, four, 0)


def kernel(
    info, xpa, xpb, xda, xdb, wq, wkv, wt, cache,
    opa, opb, oda, odb,
    gpa, gpb, gda, gdb, w, accp, accd, takep, taked, tok, s1, r1, r2, qj, qh,
    kvown, k1, k2, att, heads, dec, ppa, ppb, pda, pdb, lpa, lpb, lda, ldb,
    send, recv, gsend, grecv, asend, arecv, ksend, krecv, hsend, hrecv, osend, orecv,
):
    gx, x, z, yl = place()
    yz = lax.axis_index("yz")
    own = dict(zip(KINDS, (xpa, xpb, xda, xdb)))
    got = dict(zip(KINDS, (gpa, gpb, gda, gdb)))
    result = dict(zip(KINDS, (opa, opb, oda, odb)))
    held = dict(zip(KINDS, (ppa, ppb, pda, pdb)))
    landing = dict(zip(KINDS, (lpa, lpb, lda, ldb)))
    acc = {"p": accp, "d": accd}
    take = {"p": takep, "d": taked}
    pending = []

    def near(d):
        dx = {"x+": 1, "x-": X - 1}.get(d, 0)
        dz = {"z+": 1, "z-": Z - 1}.get(d, 0)
        return (gx, flat((x + dx) % X, (z + dz) % Z, yl))

    z_peers = [(gx, flat(x, (z + s) % Z, yl)) for s in range(1, Z)]
    xy_peers = [(gx, flat((x + e // 2) % X, z, (yl + e) % YL)) for e in range(1, X * YL)]
    g_peers = [((gx + s) % GX, yz) for s in range(1, GX)]

    def remote(src, dst, ssem, rsem, device):
        return pltpu.make_async_remote_copy(
            src_ref=src, dst_ref=dst, send_sem=ssem, recv_sem=rsem, device_id=device, device_id_type=MESH
        )

    def start(src, dst, ssem, rsem, device):
        c = remote(src, dst, ssem, rsem, device)
        c.start()
        pending.append(c)

    def arrive(dst, ssem, rsem):
        remote(dst, dst, ssem, rsem, near("x+")).wait_recv()

    barrier = pltpu.get_barrier_semaphore()
    peers = z_peers + xy_peers + g_peers
    for peer in peers:
        pl.semaphore_signal(barrier, inc=1, device_id=peer, device_id_type=MESH)
    pl.semaphore_wait(barrier, len(peers))

    tok[...] = jnp.zeros(tok.shape, F32)
    qj[...] = jnp.zeros(qj.shape, F32)

    def slot(key, rows):
        kind, xo, zo = key
        first = pl.multiple_of(((z + zo) % Z) * BLK + rows[0], 16)
        return got[kind].at[(x + xo) % X, pl.ds(first, rows[1])]

    seen = {}

    def multiply(kind, xo):
        xx = (x + xo) % X
        part = lax.dot_general(
            w[pl.ds(pl.multiple_of(xx * (Z * BLK), 128), Z * BLK), :],
            got[kind][xx],
            (((0,), (0,)), ((), ())),
            preferred_element_type=F32,
        )
        lanes = slice(START[kind], START[kind] + WIDTH[kind])
        if kind in seen:
            acc[kind[0]][:, lanes] += part
        else:
            acc[kind[0]][:, lanes] = part
            seen[kind] = True

    def gather_node(key):
        kind, xo, zo = key
        mine = (xo, zo) == (0, 0)
        if not mine:
            for _, rows in IN.pieces[key]:
                k = IN.fills[(key, rows)]
                arrive(slot(key, rows), send.at[k], recv.at[k])
        for n, (d, rows, there) in enumerate(steps_from(key)):
            k = IN.sends[(key, n)]
            start(
                own[kind] if mine else slot(key, rows),
                slot(key, rows),
                send.at[k],
                recv.at[k],
                near(d),
            )
        if mine:
            first = pl.multiple_of(z * BLK, 16)
            got[kind][x, pl.ds(first, BLK), :] = own[kind][...]
        seen[(kind, xo)] = seen.get((kind, xo), 0) + 1
        if seen[(kind, xo)] == Z:
            multiply(kind, xo)

    def sum_start(f):
        for s in range(1, GX):
            to = (gx + s) % GX
            lane = pl.multiple_of(to * 128, 128)
            start(
                acc[f].at[pl.ds(0, ROWS1), pl.ds(lane, 128)],
                take[f].at[s - 1],
                gsend.at[n_of[f], s],
                grecv.at[n_of[f], s],
                g_peers[s - 1],
            )

    n_of = {"p": 0, "d": 1}

    def exchange_z(i):
        for s in range(1, Z):
            start(
                s1.at[i, :, (z + s) % Z],
                r1.at[i, :, z],
                asend.at[i, s],
                arecv.at[i, s],
                z_peers[s - 1],
            )
        r1[i, :, z] = s1[i, :, z]

    def exchange_xy(i):
        for s in range(1, Z):
            arrive(r1.at[i, :, (z + Z - s) % Z], asend.at[i, s], arecv.at[i, s])
        for e in range(1, X * YL):
            start(
                r1.at[i, (x + e // 2) % X, :, (yl + e) % YL],
                r2.at[i, x, :, yl],
                asend.at[i, Z + e],
                arecv.at[i, Z + e],
                xy_peers[e - 1],
            )
        r2[i, x, :, yl] = r1[i, x, :, yl]

    def exchange_end(i):
        for e in range(1, X * YL):
            arrive(
                r2.at[i, (x + X - e // 2) % X, :, (yl + e) % YL], asend.at[i, Z + e], arecv.at[i, Z + e]
            )

    def token(f, xx, zz, yy, t):
        r = flat(xx, zz, yy)
        return 2 * r + t if f == "p" else t * 64 + r

    def queries_start(f):
        for s in range(1, GX):
            arrive(take[f].at[s - 1], gsend.at[n_of[f], s], grecv.at[n_of[f], s])
        lane = pl.multiple_of(gx * 128, 128)
        total = acc[f][:ROWS1, pl.ds(lane, 128)]
        for s in range(1, GX):
            total = total + take[f][s - 1]
        total = total.astype(BF16).astype(F32)
        tok[:, :ROWS1] = total.T
        i = 2 * n_of[f]

        def pack(xx, zz, yy, g, j):
            for t in range(2):
                s1[i, xx, zz, yy, pl.ds(t, 1), :] = tok[pl.ds(token(f, xx, zz, yy, t), 1), :]

        copy_rows(pack)
        exchange_z(i)
        if f == "p":
            kvown[...] = total[COLS : COLS + KVC]
            for s in range(1, Z):
                start(kvown, k1.at[z], ksend.at[s], krecv.at[s], z_peers[s - 1])
            k1[z] = kvown[...]

    def queries_pass(f):
        exchange_xy(2 * n_of[f])
        if f == "p":
            for s in range(1, Z):
                arrive(k1.at[(z + Z - s) % Z], ksend.at[s], krecv.at[s])
            for e in range(1, X * YL):
                start(k1, k2.at[x, :, yl], ksend.at[Z + e], krecv.at[Z + e], xy_peers[e - 1])
            k2[x, :, yl] = k1[...]

    nt = (((1,), (1,)), ((), ()))
    scale = HD ** (-0.5)

    def attend(f):
        i = 2 * n_of[f]
        exchange_end(i)

        def unpack(xx, zz, yy, g, j):
            for t in range(2):
                qj[j, pl.ds(t * 16 + g, 1), :] = r2[i, xx, zz, yy, pl.ds(t, 1), :]

        copy_rows(unpack)
        qh[0:32, :192] = qj[0, :, :192]
        qh[0:32, 192:] = qj[1, :, :64]
        qh[32:64, :128] = qj[1, :, 64:192]
        qh[32:64, 128:] = qj[2, :, :128]
        qh[64:96, :64] = qj[2, :, 128:192]
        qh[64:96, 64:] = qj[3, :, :192]
        q32 = qh[...]
        q = q32.astype(BF16)
        if f == "p":
            for e in range(1, X * YL):
                arrive(k2.at[(x + X - e // 2) % X, :, (yl + e) % YL], ksend.at[Z + e], krecv.at[Z + e])
            kvt = k2[...].reshape(2 * HD, PLEN).astype(BF16)
            s = jnp.dot(q, kvt[:HD], preferred_element_type=F32) * scale
            query = 2 * yz + (lax.broadcasted_iota(jnp.int32, s.shape, 0) // 16) % 2
            pos = lax.broadcasted_iota(jnp.int32, s.shape, 1)
            s = jnp.where((pos <= query) & (pos < info[1]), s, -1e30)
            e = jnp.exp(s - jnp.max(s, axis=1, keepdims=True))
            probs = (e / jnp.sum(e, axis=1, keepdims=True)).astype(BF16)
            out = lax.dot_general(probs, kvt[HD:], nt, preferred_element_type=F32)
        else:
            row = lax.broadcasted_iota(jnp.int32, (KVC, 2 * HD), 0)
            lane = lax.broadcasted_iota(jnp.int32, (KVC, 2 * HD), 1)
            spread = (lane % KVC == row).astype(BF16)
            group = lax.broadcasted_iota(jnp.int32, (32, 2 * HD), 0) % 16
            holder = lax.broadcasted_iota(jnp.int32, (32, 2 * HD), 1) // KVC
            new = jnp.zeros((32, 2 * HD), F32)
            for j in range(4):
                wide = jnp.dot(
                    qj[j, :, COLS : COLS + KVC].astype(BF16), spread, preferred_element_type=F32
                )
                new = new + jnp.where(holder == 4 * group + j, wide, 0.0)
            new0 = jnp.sum(new[:16], axis=0, keepdims=True)
            new1 = jnp.sum(new[16:], axis=0, keepdims=True)
            s = lax.dot_general(q, cache[:, :HD], nt, preferred_element_type=F32) * scale
            pos = lax.broadcasted_iota(jnp.int32, s.shape, 1)
            s = jnp.where(pos < info[0], s, -1e30)
            f0 = jnp.sum(q32 * new0[:, :HD], axis=1, keepdims=True) * scale
            f1 = jnp.sum(q32 * new1[:, :HD], axis=1, keepdims=True) * scale
            step = (lax.broadcasted_iota(jnp.int32, f1.shape, 0) // 16) % 2
            f1 = jnp.where(step == 1, f1, -1e30)
            peak = jnp.maximum(jnp.max(s, axis=1, keepdims=True), jnp.maximum(f0, f1))
            es, e0, e1 = jnp.exp(s - peak), jnp.exp(f0 - peak), jnp.exp(f1 - peak)
            total = jnp.sum(es, axis=1, keepdims=True) + e0 + e1
            out = jnp.dot((es / total).astype(BF16), cache[:, HD:], preferred_element_type=F32)
            out = out + (e0 / total).astype(BF16).astype(F32) * new0[:, HD:]
            out = out + (e1 / total).astype(BF16).astype(F32) * new1[:, HD:]
        qh[...] = out.astype(BF16).astype(F32)
        qj[0, :, :192] = qh[0:32, :192]
        qj[1, :, :64] = qh[0:32, 192:]
        qj[1, :, 64:192] = qh[32:64, :128]
        qj[2, :, :128] = qh[32:64, 128:]
        qj[2, :, 128:192] = qh[64:96, :64]
        qj[3, :, :192] = qh[64:96, 64:]

        def pack(xx, zz, yy, g, j):
            for t in range(2):
                s1[i + 1, xx, zz, yy, pl.ds(t, 1), :] = qj[j, pl.ds(t * 16 + g, 1), :]

        copy_rows(pack)
        exchange_z(i + 1)

    def attended_pass(f):
        exchange_xy(2 * n_of[f] + 1)

    def attended_share(f):
        n = n_of[f]
        i = 2 * n + 1
        exchange_end(i)

        def unpack(xx, zz, yy, g, j):
            for t in range(2):
                tok[pl.ds(token(f, xx, zz, yy, t), 1), :] = r2[i, xx, zz, yy, pl.ds(t, 1), :]

        copy_rows(unpack)
        att[n] = tok[...].T[:COLS].astype(BF16)
        for s in range(1, GX):
            start(att.at[n], heads.at[n, s], hsend.at[n, s], hrecv.at[n, s], g_peers[s - 1])
        heads[n, 0] = att[n]

    def attended_end(f):
        n = n_of[f]
        for s in range(1, GX):
            arrive(heads.at[n, s], hsend.at[n, s], hrecv.at[n, s])
        if f == "d":
            for s in range(GX):
                lane = pl.multiple_of(((gx - s + GX) % GX) * 128, 128)
                dec[:, pl.ds(lane, 128)] = heads[n, s]

    def terms(key):
        kind, xo, zo = key
        xx, zz = (x + xo) % X, (z + zo) % Z
        if kind[0] == "d":
            first = pl.multiple_of((xx * Z + zz) * BLK, 16)
            lanes = slice(START[kind], START[kind] + WIDTH[kind])
            return jnp.dot(wt[pl.ds(first, BLK), :], dec[:, lanes], preferred_element_type=F32)
        group = heads[0, (gx - xx + GX) % GX]
        parts = []
        for q in range(START[kind] // 128, (START[kind] + WIDTH[kind]) // 128):
            first = pl.multiple_of(zz * (4 * BLK) + q * BLK, 16)
            parts.append(jnp.dot(wt[pl.ds(first, BLK), :], group, preferred_element_type=F32))
        return jnp.concatenate(parts, axis=1)

    def scatter_node(key):
        kind, xo, zo = key
        last = (xo, zo) == (0, 0)
        at = ((x + xo) % X) * Z + (z + zo) % Z
        local = terms(key)
        steps = steps_from(key)
        for n, (d, rows, there) in enumerate(steps):
            k = OUT.sends[(key, n)]
            spot = landing[kind].at[OUT.where[(key, n)], pl.ds(rows[0], rows[1])]
            arrive(spot, osend.at[k], orecv.at[k])
        halves = [local[:80], local[80:]]
        for n, (d, rows, there) in enumerate(steps):
            for i, (r0, rn) in enumerate((UPPER, LOWER)):
                if rows[0] <= r0 and r0 + rn <= rows[0] + rows[1]:
                    halves[i] = halves[i] + landing[kind][OUT.where[(key, n)], r0 : r0 + rn].astype(F32)
        for i, (r0, rn) in enumerate((UPPER, LOWER)):
            if last:
                result[kind][r0 : r0 + rn] = halves[i]
            else:
                held[kind][at, r0 : r0 + rn] = halves[i].astype(BF16)
        if not last:
            for d, rows in OUT.pieces[key]:
                k = OUT.fills[(key, rows)]
                start(
                    held[kind].at[at, pl.ds(rows[0], rows[1])],
                    landing[kind].at[OUT.where[OUT.source[k]], pl.ds(rows[0], rows[1])],
                    osend.at[k],
                    orecv.at[k],
                    near(OPPOSITE[d]),
                )

    middle = [sum_start, queries_start, queries_pass, attend, attended_pass, attended_share]

    prefill_done = max(IN.times[key] for key in IN.order if key[0][0] == "p")
    todo = [(prefill_done + 4.0 * n, step) for n, step in enumerate(middle)]
    for key in IN.order:
        while todo and IN.times[key] > todo[0][0]:
            todo.pop(0)[1]("p")
        gather_node(key)
        if key == ("da", 0, 0):
            w[:, :COLS] = wq[...]
            w[:, COLS:] = jnp.zeros((wq.shape[0], 256 - COLS), BF16)
            w[:, COLS : COLS + KVC] = wkv[...]
    sum_start("d")
    for _, step in todo:
        step("p")
    attended_end("p")

    todo = [(4.0 * n, step) for n, step in enumerate(middle)][1:]
    todo.append((24.0, attended_end))
    for key in reversed(OUT.order):
        while todo and (OUT.end - OUT.times[key] > todo[0][0] or key[0][0] == "d"):
            todo.pop(0)[1]("d")
        scatter_node(key)
    for c in pending:
        c.wait_send()


def run(info, xpa, xpb, xda, xdb, wq, wkv, wt, cache):
    vmem = pl.BlockSpec(memory_space=pltpu.VMEM)
    dma = pltpu.SemaphoreType.DMA
    return pl.pallas_call(
        kernel,
        out_shape=tuple(jax.ShapeDtypeStruct((BLK, WIDTH[k]), F32) for k in KINDS),
        in_specs=[pl.BlockSpec(memory_space=pltpu.SMEM)] + [vmem] * 8,
        out_specs=(vmem,) * 4,
        scratch_shapes=[pltpu.VMEM((X, Z * BLK, WIDTH[k]), BF16) for k in KINDS]
        + [
            pltpu.VMEM((wq.shape[0], 256), BF16),
            pltpu.VMEM((256, TOK), F32),
            pltpu.VMEM((256, TOK), F32),
            pltpu.VMEM((GX - 1, ROWS1, 128), F32),
            pltpu.VMEM((GX - 1, ROWS1, 128), F32),
            pltpu.VMEM((128, 256), F32),
            pltpu.VMEM((4, X, Z, YL, 2, 256), F32),
            pltpu.VMEM((4, X, Z, YL, 2, 256), F32),
            pltpu.VMEM((4, X, Z, YL, 2, 256), F32),
            pltpu.VMEM((4, 32, 256), F32),
            pltpu.VMEM((96, 256), F32),
            pltpu.VMEM((KVC, PLEN), F32),
            pltpu.VMEM((Z, KVC, PLEN), F32),
            pltpu.VMEM((X, Z, YL, KVC, PLEN), F32),
            pltpu.VMEM((2, COLS, 128), BF16),
            pltpu.VMEM((2, GX, COLS, 128), BF16),
            pltpu.VMEM((COLS, TOK), BF16),
        ]
        + [pltpu.VMEM((X * Z, BLK, WIDTH[k]), BF16) for k in KINDS]
        + [pltpu.VMEM((OUT.slots[k], BLK, WIDTH[k]), BF16) for k in KINDS]
        + [
            dma((NSEND,)),
            dma((NSEND,)),
            dma((2, GX)),
            dma((2, GX)),
            dma((4, 16)),
            dma((4, 16)),
            dma((16,)),
            dma((16,)),
            dma((2, GX)),
            dma((2, GX)),
            dma((NSEND,)),
            dma((NSEND,)),
        ],
        compiler_params=pltpu.CompilerParams(
            collective_id=0, has_side_effects=True, vmem_limit_bytes=58 * 2**20
        ),
        name="attention_block",
    )(info, xpa, xpb, xda, xdb, wq, wkv, wt, cache)


def body(
    prefill_tokens,
    prefill_lengths,
    decode_tokens,
    cache_lengths,
    cache_keyvals,
    query_weight,
    keyval_weight,
    out_weight,
):
    gx, x, z, yl = place()
    group = query_weight.shape[0]
    slices = [
        lax.dynamic_slice(prefill_tokens, (0, g * group + (x * Z + z) * BLK), (PLEN, BLK)).T
        for g in range(GX)
    ]
    pre = lax.all_to_all(jnp.stack(slices), "gx", split_axis=0, concat_axis=0, tiled=True)
    pre = pre.transpose(1, 0, 2).reshape(BLK, GX * PLEN)
    dec = decode_tokens.reshape(2, GX, 64, 72).transpose(3, 1, 0, 2).reshape(72, 512)
    other = lax.ppermute(dec, "yz", [(i, i ^ 1) for i in range(X * Z * YL)])
    dec = jnp.where(
        yl == 0, jnp.concatenate([dec, other], axis=0), jnp.concatenate([other, dec], axis=0)
    )
    split = WIDTH["pa"], WIDTH["da"]
    info = jnp.stack([cache_lengths[0], prefill_lengths[0]]).astype(jnp.int32)
    opa, opb, oda, odb = run(
        info,
        pre[:, : split[0]],
        pre[:, split[0] :],
        dec[:, : split[1]],
        dec[:, split[1] :],
        query_weight,
        keyval_weight,
        out_weight.T,
        cache_keyvals[0],
    )

    pre = jnp.concatenate([opa, opb], axis=1)
    dec = jnp.concatenate([oda, odb], axis=1)
    swap = [(i, i ^ 1) for i in range(X * Z * YL)]
    dec_other = lax.ppermute(jnp.where(yl == 0, dec[72:], dec[:72]), "yz", swap)
    pre_other = lax.ppermute(jnp.where(yl == 0, pre[:, 256:], pre[:, :256]), "yz", swap)
    dec = jnp.where(yl == 0, dec[:72], dec[72:]) + dec_other
    pre = jnp.where(yl == 0, pre[:, :256], pre[:, 256:]) + pre_other
    decode_out = dec.reshape(72, GX, 2, 64).transpose(2, 1, 3, 0).reshape(2, 256, 72)
    turn = []
    for g in range(GX):
        for i in range(X * Z * YL):
            turn.append((g * 64 + i, (i // 16) * 64 + g * 16 + i % 16))
    pre = lax.ppermute(pre.astype(BF16), ("gx", "yz"), turn)
    prefill_out = pre.reshape(BLK, 2, PLEN).transpose(2, 1, 0).reshape(PLEN, 2 * BLK)
    return (prefill_out, decode_out.astype(BF16))


def solution(mesh):
    in_specs = (
        P("gx", None),
        P("gx"),
        P(None, None, ("gx", "yz")),
        P(("gx", "yz")),
        P(("gx", "yz"), None, None),
        P("gx", "yz"),
        P("gx", "yz"),
        P("yz", "gx"),
    )
    out_specs = (P("gx", "yz"), P(None, None, ("gx", "yz")))
    return jax.shard_map(body, mesh=mesh, in_specs=in_specs, out_specs=out_specs, check_vma=False)
```

time: 1860 us -> 235 us (0.13)
  waiting for transfers between devices: 1510 us -> 6.13 us
  blocking collectives: 222 us -> 0 us
  Pallas kernels: 0 us -> 189 us
  matrix products: 49.3 us -> 0 us
  starting transfers between devices: 45.2 us -> 14.8 us
    reduce_scatter x5 -> x0, waiting for transfers between devices: 848 us -> none  [the longest x2 496 us: project_outputs(): lax.psum_scatter(partial_terms, 'yz', scatter_dimension=1, tiled=True)]
    all_gather x4 -> x0, waiting for transfers between devices: 603 us -> none  [the longest x2 603 us: project_inputs(): portion = lax.all_gather(rows_input, 'yz', axis=1, tiled=True)]
    pallas_call x0 -> x1, Pallas kernels: none -> 189 us  [run(): pl.pallas_call(kernel, out_shape=tuple((jax.ShapeDtypeStruct((BLK, WIDTH[...]
    all_gather x4 -> x0, blocking collectives: 179 us -> none  [the longest x1 157 us: body(): keyval_all = lax.all_gather(keyval_local, 'yz', axis=1, tiled=True)]
    all_to_all x3 -> x0, blocking collectives: 43.1 us -> none  [the longest x2 28.7 us: project_outputs(): lax.all_to_all(attended_rows, 'yz', split_axis=1, concat_axis=0, tiled=True)]
    dot_general x16 -> x0, matrix products: 43 us -> none  [the longest x1 10.4 us: body(): jnp.dot(returned, lax.all_gather(out_weight, 'gx', axis=1, tiled=True), p...]
    unnamed x13 -> x0, waiting for transfers between devices: 40.4 us -> none
    all_to_all x5 -> x1, starting transfers between devices: 44.5 us -> 4.8 us  [body(): lax.all_to_all(jnp.stack(slices), 'gx', split_axis=0, concat_axis=0, tile...]
  transfers between devices with their start and end apart: 16 -> 5, of which waited for: 10 -> 2; matrix products, arithmetic and copies ran while one was open for 3% -> 6% of each run, Pallas kernels for 0% -> 0%
where the time goes in v2:
time: 235 us; the launch traced here: 232 us
  Pallas kernels  189 us (80%)
  local copies, waits for them, and re-layouts  16.3 us (7%)
  starting transfers between devices  14.8 us (6%)
  waiting for transfers between devices  6.13 us (3%)
  other arithmetic  4.26 us (2%)
    pallas_call x1, Pallas kernels, run(): pl.pallas_call(kernel, out_shape=tuple((jax.ShapeDtypeStruct((BLK, WIDTH[...  189 us
    unnamed x14, local copies, waits for them, and re-layouts  7.67 us
    ppermute x1, starting transfers between devices, body(): pre = lax.ppermute(pre.astype(BF16), ('gx', 'yz'), turn)  6.55 us
    all_to_all x1, starting transfers between devices, body(): lax.all_to_all(jnp.stack(slices), 'gx', split_axis=0, concat_axis=0, tile...  4.8 us
  transfers between devices with their start and end apart: 5, of which 2 were waited for; matrix products, arithmetic and copies ran while one was open for 6% of the time, Pallas kernels for 0%

profile of v2, /device:TPU:16, one launch (start us, length us, event | category | flops | bytes accessed | tf_op | source)
XLA Modules:
  0.0 232.4 jit_solution(8637179645477763501)
XLA Ops:
  0.7 1.1 reshape.24
  1.9 0.8 reshape.25
  2.7 1.3 collective-permute-start
  4.0 1.2 constant_dynamic-slice_fusion.3
  5.6 0.7 pad_maximum_fusion
  6.3 4.8 %all-to-all-start = ((bf16[4,144,128]{2,1,0:T(8,128)(2,1)}), bf16[4,144,128]{2,1,0:T(8,128)(2,1)}, u32[]{:S(2)}, u32[]{:S(2)}) async-start(bf16[4,144,128]{2,1,0:T(8,128)(2,1)} %pad_maximum_fusion), calls=%async_computation | async-start | bytes 294912 | tf_op jit(solution)/shard_map/all_to_all | solution.py:532
  12.4 1.4 copy.32.wkv
  13.9 2.4 %copy.31.wq = bf16[4608,192]{1,0:T(8,128)(2,1)} copy(bf16[4608,192]{0,1:T(8,128)(2,1)S(1)} %copy-done) | data formatting | bytes 3538944 | tf_op args[5]
  16.3 2.4 %copy.30 = bf16[192,4608]{0,1:T(8,128)(2,1)} copy(bf16[192,4608]{1,0:T(8,128)(2,1)S(1)} %copy-done.1) | data formatting | bytes 3538944 | tf_op args[7]
  19.3 1.0 maximum_select_fusion
  20.9 0.7 slice.28.xda
  21.6 0.9 copy_bitcast_fusion
  22.5 0.7 fusion
  23.2 188.9 %attention_block.1 = (f32[144,256]{1,0:T(8,128)}, f32[144,256]{1,0:T(8,128)}, f32[144,384]{1,0:T(8,128)}, f32[144,128]{1,0:T(8,128)}) custom-call(s32[2]{0:T(128)} %pad_add_fusion.info, bf16[144,256]{1,0:T(8,128)(2,1)} %get-tuple-element.15.xpa, bf16[144,256]{1,0:T(8,128)(2,1)} %get-tuple-element.14.xpb, bf16[144,384]{1,0:T(8,128)(2,1)} %slice.28.xda, ...), custom_call_target="tpu_custom_call" | custom-call | tf_op jit(solution)/shard_map/attention_block/pallas_call | solution.py:468
  212.1 1.0 constant_dynamic-update-slice_fusion.1
  213.0 0.9 broadcast_select_fusion
  214.0 1.2 collective-permute-start.1
  215.2 0.9 constant_dynamic-update-slice_fusion
  216.1 1.0 collective-permute-start.3
  217.1 3.6 %collective-permute-done.1 = f32[144,256]{1,0:T(8,128)S(1)} collective-permute-done((f32[144,256]{1,0:T(8,128)S(1)}, f32[144,256]{1,0:T(8,128)S(1)}, u32[]{:S(2)}, u32[]{:S(2)}) %collective-permute-start.1) | collective-permute-done | bytes 147488 | tf_op jit(solution)/shard_map/ppermute | solution.py:557
  220.6 0.9 add_convert_fusion.1
  221.6 6.6 %collective-permute-start.2 = (bf16[144,256]{1,0:T(8,128)(2,1)S(1)}, bf16[144,256]{1,0:T(8,128)(2,1)S(1)}, u32[]{:S(2)}, u32[]{:S(2)}) collective-permute-start(bf16[144,256]{1,0:T(8,128)(2,1)S(1)} %add_convert_fusion.1), channel_id=1, source_target_pairs={{0,0},{1,1},{2,2},{3,3},{4,4},{5,5},{6,6},{7,7},{8,8},{9,9},{10,10... | collective-permute-start | bytes 221192 | tf_op jit(solution)/shard_map/ppermute | solution.py:565
  228.4 0.8 convert_element_type.19
  229.2 2.6 %collective-permute-done.2 = bf16[144,256]{1,0:T(8,128)(2,1)S(1)} collective-permute-done((bf16[144,256]{1,0:T(8,128)(2,1)S(1)}, bf16[144,256]{1,0:T(8,128)(2,1)S(1)}, u32[]{:S(2)}, u32[]{:S(2)}) %collective-permute-start.2) | collective-permute-done | bytes 73760 | tf_op jit(solution)/shard_map/ppermute | solution.py:565
  (22 shorter events, 2.7 us)
Async XLA Ops:
  0.6 11.8 %copy-start.2 = (bf16[4608,8]{0,1:T(8,128)(2,1)S(1)}, bf16[4608,8]{0,1:T(8,128)(2,1)}, u32[]{:S(2)}) copy-start(bf16[4608,8]{0,1:T(8,128)(2,1)} %param.14) | copy-start | bytes 221188
  0.6 13.3 %copy-start = (bf16[4608,192]{0,1:T(8,128)(2,1)S(1)}, bf16[4608,192]{0,1:T(8,128)(2,1)}, u32[]{:S(2)}) copy-start(bf16[4608,192]{0,1:T(8,128)(2,1)} %param.13) | copy-start | bytes 5308420
  2.7 16.6 %collective-permute-start = (bf16[72,512]{1,0:T(8,128)(2,1)}, bf16[72,512]{1,0:T(8,128)(2,1)}, u32[]{:S(2)}, u32[]{:S(2)}) collective-permute-start(bf16[72,512]{1,0:T(8,128)(2,1)} %reshape.25), channel_id=1, source_target_pairs={{0,1},{1,0},{2,3},{3,2},{4,5},{5,4},{6,7},{7,6},{8,9},{9,8},{10,11... | collective-permute-start | bytes 221192 | tf_op jit(solution)/shard_map/ppermute | solution.py:535
  6.3 15.3 %all-to-all-start = ((bf16[4,144,128]{2,1,0:T(8,128)(2,1)}), bf16[4,144,128]{2,1,0:T(8,128)(2,1)}, u32[]{:S(2)}, u32[]{:S(2)}) async-start(bf16[4,144,128]{2,1,0:T(8,128)(2,1)} %pad_maximum_fusion), calls=%async_computation | async-start | bytes 294912 | tf_op jit(solution)/shard_map/all_to_all | solution.py:532
  13.9 2.4 %copy-start.1 = (bf16[192,4608]{1,0:T(8,128)(2,1)S(1)}, bf16[192,4608]{1,0:T(8,128)(2,1)}, u32[]{:S(2)}) copy-start(bf16[192,4608]{1,0:T(8,128)(2,1)} %param.15) | copy-start | bytes 5308420
  214.0 6.7 %collective-permute-start.1 = (f32[144,256]{1,0:T(8,128)S(1)}, f32[144,256]{1,0:T(8,128)S(1)}, u32[]{:S(2)}, u32[]{:S(2)}) collective-permute-start(f32[144,256]{1,0:T(8,128)S(1)} %broadcast_select_fusion), channel_id=1, source_target_pairs={{0,1},{1,0},{2,3},{3,2},{4,5},{5,4},{6,7},{7,6},{8,9},{9,8},{10,11... | collective-permute-start | bytes 442376 | tf_op jit(solution)/shard_map/ppermute | solution.py:557
  216.1 12.1 %collective-permute-start.3 = (f32[72,512]{1,0:T(8,128)S(1)}, f32[72,512]{1,0:T(8,128)S(1)}, u32[]{:S(2)}, u32[]{:S(2)}) collective-permute-start(f32[72,512]{1,0:T(8,128)S(1)} %slice_select_fusion), channel_id=1, source_target_pairs={{0,1},{1,0},{2,3},{3,2},{4,5},{5,4},{6,7},{7,6},{8,9},{9,8},{10,11... | collective-permute-start | bytes 442376 | tf_op jit(solution)/shard_map/ppermute | solution.py:556
  221.6 10.2 %collective-permute-start.2 = (bf16[144,256]{1,0:T(8,128)(2,1)S(1)}, bf16[144,256]{1,0:T(8,128)(2,1)S(1)}, u32[]{:S(2)}, u32[]{:S(2)}) collective-permute-start(bf16[144,256]{1,0:T(8,128)(2,1)S(1)} %add_convert_fusion.1), channel_id=1, source_target_pairs={{0,0},{1,1},{2,2},{3,3},{4,4},{5,5},{6,6},{7,7},{8,8},{9,9},{10,10... | collective-permute-start | bytes 221192 | tf_op jit(solution)/shard_map/ppermute | solution.py:565

commit v3 on v2

--- a/solution.py
+++ b/solution.py
@@ -13,9 +13,10 @@
 GX, X, Z, YL = 4, 4, 8, 2
 BLK = 144
 TOK = 512
-WIDTH = {"pa": 256, "pb": 256, "da": 384, "db": 128}
+WIDTH_IN = {"pa": 128, "pb": 128, "da": 384, "db": 128}
+WIDTH_OUT = {"pa": 256, "pb": 256, "da": 384, "db": 128}
 START = {"pa": 0, "pb": 256, "da": 0, "db": 384}
-KINDS = tuple(WIDTH)
+KINDS = tuple(START)
 COLS = 192
 KVC = 8
 ROWS1 = 208
@@ -62,7 +63,7 @@
 
 
 class Plan:
-    def __init__(self, kinds):
+    def __init__(self, kinds, width, later):
         free = dict.fromkeys(OPPOSITE, 0.0)
         events, self.order, self.times, self.pieces = [], [], {}, {}
         self.sends, self.fills, self.source, self.where = {}, {}, {}, {}
@@ -72,7 +73,7 @@
             self.order.append(key)
             self.times[key] = now
             for n, (d, rows, there) in enumerate(steps_from(key)):
-                free[d] = max(free[d], now) + WIDTH[key[0]] * rows[1] * 4e-5
+                free[d] = max(free[d], now) + width[key[0]] * rows[1] * 4e-5
                 k = len(self.sends)
                 self.sends[(key, n)] = k
                 self.fills[(there, rows)] = k
@@ -81,19 +82,21 @@
                 self.slots[key[0]] += 1
                 heapq.heappush(events, (free[d] + 1.0, k, there, (d, rows)))
 
-        for kind in kinds:
-            leave((kind, 0, 0), 0.0)
+        for n, kind in enumerate(kinds):
+            release = later if kind[0] != kinds[0][0] else 0.0
+            heapq.heappush(events, (release, n - len(kinds), (kind, 0, 0), None))
         while events:
             now, _, key, piece = heapq.heappop(events)
-            self.pieces.setdefault(key, []).append(piece)
-            if sum(p[1][1] for p in self.pieces[key]) == BLK:
+            if piece is not None:
+                self.pieces.setdefault(key, []).append(piece)
+            if piece is None or sum(p[1][1] for p in self.pieces[key]) == BLK:
                 leave(key, now)
         assert len(self.order) == X * Z * len(kinds)
         self.end = max(self.times.values())
 
 
-IN = Plan(("pb", "pa", "db", "da"))
-OUT = Plan(("db", "da", "pb", "pa"))
+IN = Plan(("pb", "pa", "db", "da"), WIDTH_IN, 12.0)
+OUT = Plan(("db", "da", "pb", "pa"), WIDTH_OUT, 22.0)
 NSEND = len(IN.sends)
 
 
@@ -117,14 +120,18 @@
 
 
 def kernel(
-    info, xpa, xpb, xda, xdb, wq, wkv, wt, cache,
-    opa, opb, oda, odb,
-    gpa, gpb, gda, gdb, w, accp, accd, takep, taked, tok, s1, r1, r2, qj, qh,
-    kvown, k1, k2, att, heads, dec, ppa, ppb, pda, pdb, lpa, lpb, lda, ldb,
-    send, recv, gsend, grecv, asend, arecv, ksend, krecv, hsend, hrecv, osend, orecv,
+    info, dtok, wkv, ptok, wq, wo, cache_hbm,
+    prefill_out, decode_out,
+    gpa, gpb, gda, gdb, w, wov, wt, cache, tloc, win, winT, xpa, xpb, xda, xdb, dsend, drecv,
+    accp, accd, takep, taked, tok, s1, r1, r2, qj, qh,
+    kvown, k1, k2, att, heads, dec, dec2, ppa, ppb, pda, pdb, lpa, lpb, lda, ldb,
+    opa, opb, oda, odb, psend, precv, dsend2, drecv2, pfin, pland,
+    local, esend, erecv, send, recv, gsend, grecv, asend, arecv, ksend, krecv, hsend, hrecv,
+    osend, orecv, fsend, frecv,
 ):
     gx, x, z, yl = place()
     yz = lax.axis_index("yz")
+    core, y_hi = gx % 2, gx // 2
     own = dict(zip(KINDS, (xpa, xpb, xda, xdb)))
     got = dict(zip(KINDS, (gpa, gpb, gda, gdb)))
     result = dict(zip(KINDS, (opa, opb, oda, odb)))
@@ -158,34 +165,96 @@
 
     barrier = pltpu.get_barrier_semaphore()
     peers = z_peers + xy_peers + g_peers
+    keeper = (x, flat(gx, z, yl))
+    turned = x != gx
     for peer in peers:
         pl.semaphore_signal(barrier, inc=1, device_id=peer, device_id_type=MESH)
-    pl.semaphore_wait(barrier, len(peers))
-
+
+    @pl.when(turned)
+    def _():
+        pl.semaphore_signal(barrier, inc=1, device_id=keeper, device_id_type=MESH)
+
+    group = wq.shape[1]
+    edge = (x * Z + z) * BLK
+    aligned = (edge // 128) * 128
+    loads = []
+
+    def load(src, dst):
+        c = pltpu.make_async_copy(src, dst, local.at[len(loads)])
+        c.start()
+        loads.append(c)
+        return c
+
+    there = 1 - y_hi
+    windows = []
+    for c in range(2):
+        lane = pl.multiple_of((2 * there + c) * group + aligned, 128)
+        windows.append(load(ptok.at[:, pl.ds(lane, 256)], win.at[c]))
+    w_load = load(wq, w.at[pl.ds(0, COLS)])
+    mine_load = load(ptok.at[:, pl.ds(pl.multiple_of(gx * group, 128), group)], tloc.at[0])
+    wo_load = load(wo, wov)
+    cache_load = load(cache_hbm, cache)
+    dsend[:72, :256] = dtok[0]
+    dsend[:72, 256:] = dtok[1]
+    dsend[72:, :] = jnp.zeros((8, TOK), BF16)
     tok[...] = jnp.zeros(tok.shape, F32)
     qj[...] = jnp.zeros(qj.shape, F32)
+    for c in range(2):
+        windows[c].wait()
+        winT[c] = win[c].T
+    pl.semaphore_wait(barrier, len(peers) + turned.astype(jnp.int32))
+
+    partner = (gx, flat(x, z, 1 - yl))
+    first = pl.multiple_of(edge - aligned, 16)
+    landed = (xpa, xpb)
+    for c in range(2):
+
+        @pl.when(core == c)
+        def _(c=c):
+            for o in range(2):
+                remote(
+                    winT.at[o, pl.ds(first, BLK)],
+                    landed[c],
+                    esend.at[o],
+                    erecv.at[c],
+                    (2 * there + o, yz),
+                ).start()
+
+    start(dsend, drecv, esend.at[2], erecv.at[2], partner)
+    lane = pl.multiple_of((gx + 1 - 2 * core) * group, 128)
+    start(
+        ptok.at[:, pl.ds(lane, group)], tloc.at[1], esend.at[3], erecv.at[3], (gx + 1 - 2 * core, yz)
+    )
 
     def slot(key, rows):
         kind, xo, zo = key
-        first = pl.multiple_of(((z + zo) % Z) * BLK + rows[0], 16)
-        return got[kind].at[(x + xo) % X, pl.ds(first, rows[1])]
+        return got[kind].at[((x + xo) % X) * Z + (z + zo) % Z, pl.ds(rows[0], rows[1])]
 
     seen = {}
+
+    def lanes_of(kind):
+        if kind[0] == "p":
+            return pl.ds(pl.multiple_of((2 * there + "ab".index(kind[1])) * 128, 128), 128)
+        return slice(START[kind], START[kind] + WIDTH_IN[kind])
 
     def multiply(kind, xo):
         xx = (x + xo) % X
-        part = lax.dot_general(
-            w[pl.ds(pl.multiple_of(xx * (Z * BLK), 128), Z * BLK), :],
-            got[kind][xx],
-            (((0,), (0,)), ((), ())),
+        part = jnp.dot(
+            w[:, pl.ds(pl.multiple_of(xx * (Z * BLK), 128), Z * BLK)],
+            got[kind][pl.ds(xx * Z, Z)].reshape(Z * BLK, WIDTH_IN[kind]),
             preferred_element_type=F32,
         )
-        lanes = slice(START[kind], START[kind] + WIDTH[kind])
         if kind in seen:
-            acc[kind[0]][:, lanes] += part
+            acc[kind[0]][:, lanes_of(kind)] += part
         else:
-            acc[kind[0]][:, lanes] = part
+            acc[kind[0]][:, lanes_of(kind)] = part
             seen[kind] = True
+
+    def multiply_near(n):
+        lanes = pl.ds(pl.multiple_of((gx if n == 0 else gx + 1 - 2 * core) * 128, 128), 128)
+        acc["p"][:, lanes] = lax.dot_general(
+            w[...], tloc[n], (((1,), (1,)), ((), ())), preferred_element_type=F32
+        )
 
     def gather_node(key):
         kind, xo, zo = key
@@ -193,24 +262,39 @@
         if not mine:
             for _, rows in IN.pieces[key]:
                 k = IN.fills[(key, rows)]
-                arrive(slot(key, rows), send.at[k], recv.at[k])
+                arrive(slot(key, rows), send.at[KINDS.index(kind)], recv.at[k])
+        elif kind[0] == "p":
+            c = "ab".index(kind[1])
+            arrive(own[kind], esend.at[c], erecv.at[c])
+        elif kind == "db":
+            arrive(drecv, esend.at[2], erecv.at[2])
+            one, two = dsend[:72].astype(F32), drecv[:72].astype(F32)
+            both = jnp.where(
+                yl == 0, jnp.concatenate([one, two], axis=0), jnp.concatenate([two, one], axis=0)
+            ).astype(BF16)
+            xda[...] = both[:, : WIDTH_IN["da"]]
+            xdb[...] = both[:, WIDTH_IN["da"] :]
         for n, (d, rows, there) in enumerate(steps_from(key)):
             k = IN.sends[(key, n)]
-            start(
+            remote(
                 own[kind] if mine else slot(key, rows),
                 slot(key, rows),
-                send.at[k],
+                send.at[KINDS.index(kind)],
                 recv.at[k],
                 near(d),
-            )
+            ).start()
         if mine:
-            first = pl.multiple_of(z * BLK, 16)
-            got[kind][x, pl.ds(first, BLK), :] = own[kind][...]
+            got[kind][x * Z + z] = own[kind][...]
         seen[(kind, xo)] = seen.get((kind, xo), 0) + 1
         if seen[(kind, xo)] == Z:
             multiply(kind, xo)
 
     def sum_start(f):
+        if f == "d":
+            rows = accd[...]
+            for g in range(GX):
+                accd[:, g * 128 : g * 128 + 64] = rows[:, g * 64 : g * 64 + 64]
+                accd[:, g * 128 + 64 : g * 128 + 128] = rows[:, 256 + g * 64 : 320 + g * 64]
         for s in range(1, GX):
             to = (gx + s) % GX
             lane = pl.multiple_of(to * 128, 128)
@@ -388,18 +472,23 @@
         if f == "d":
             for s in range(GX):
                 lane = pl.multiple_of(((gx - s + GX) % GX) * 128, 128)
-                dec[:, pl.ds(lane, 128)] = heads[n, s]
+                dec2[:, pl.ds(lane, 128)] = heads[n, s]
+            for g in range(GX):
+                for t in range(2):
+                    dec[:, t * 256 + g * 64 : t * 256 + g * 64 + 64] = dec2[
+                        :, g * 128 + t * 64 : g * 128 + t * 64 + 64
+                    ]
 
     def terms(key):
         kind, xo, zo = key
         xx, zz = (x + xo) % X, (z + zo) % Z
         if kind[0] == "d":
             first = pl.multiple_of((xx * Z + zz) * BLK, 16)
-            lanes = slice(START[kind], START[kind] + WIDTH[kind])
+            lanes = slice(START[kind], START[kind] + WIDTH_OUT[kind])
             return jnp.dot(wt[pl.ds(first, BLK), :], dec[:, lanes], preferred_element_type=F32)
         group = heads[0, (gx - xx + GX) % GX]
         parts = []
-        for q in range(START[kind] // 128, (START[kind] + WIDTH[kind]) // 128):
+        for q in range(START[kind] // 128, (START[kind] + WIDTH_OUT[kind]) // 128):
             first = pl.multiple_of(zz * (4 * BLK) + q * BLK, 16)
             parts.append(jnp.dot(wt[pl.ds(first, BLK), :], group, preferred_element_type=F32))
         return jnp.concatenate(parts, axis=1)
@@ -413,7 +502,7 @@
         for n, (d, rows, there) in enumerate(steps):
             k = OUT.sends[(key, n)]
             spot = landing[kind].at[OUT.where[(key, n)], pl.ds(rows[0], rows[1])]
-            arrive(spot, osend.at[k], orecv.at[k])
+            arrive(spot, osend.at[KINDS.index(kind)], orecv.at[k])
         halves = [local[:80], local[80:]]
         for n, (d, rows, there) in enumerate(steps):
             for i, (r0, rn) in enumerate((UPPER, LOWER)):
@@ -427,73 +516,156 @@
         if not last:
             for d, rows in OUT.pieces[key]:
                 k = OUT.fills[(key, rows)]
-                start(
+                remote(
                     held[kind].at[at, pl.ds(rows[0], rows[1])],
                     landing[kind].at[OUT.where[OUT.source[k]], pl.ds(rows[0], rows[1])],
-                    osend.at[k],
+                    osend.at[KINDS.index(kind)],
                     orecv.at[k],
                     near(OPPOSITE[d]),
-                )
+                ).start()
 
     middle = [sum_start, queries_start, queries_pass, attend, attended_pass, attended_share]
 
+    def weights():
+        w_load.wait()
+        w[COLS:, :] = jnp.concatenate([wkv[...].astype(F32), jnp.zeros((8, group), F32)]).astype(BF16)
+        mine_load.wait()
+        multiply_near(0)
+        wo_load.wait()
+        for n in range(group // 512):
+            wt[pl.ds(512 * n, 512), :] = wov[:, 512 * n : 512 * n + 512].T
+
+    def sibling():
+        arrive(tloc.at[1], esend.at[3], erecv.at[3])
+        multiply_near(1)
+
     prefill_done = max(IN.times[key] for key in IN.order if key[0][0] == "p")
-    todo = [(prefill_done + 4.0 * n, step) for n, step in enumerate(middle)]
-    for key in IN.order:
+    todo = [(prefill_done + 3.0 * n, step) for n, step in enumerate(middle)]
+    for n, key in enumerate(IN.order):
         while todo and IN.times[key] > todo[0][0]:
             todo.pop(0)[1]("p")
         gather_node(key)
-        if key == ("da", 0, 0):
-            w[:, :COLS] = wq[...]
-            w[:, COLS:] = jnp.zeros((wq.shape[0], 256 - COLS), BF16)
-            w[:, COLS : COLS + KVC] = wkv[...]
+        if n == 1:
+            weights()
+        if n == 12:
+            sibling()
     sum_start("d")
     for _, step in todo:
         step("p")
     attended_end("p")
 
-    todo = [(4.0 * n, step) for n, step in enumerate(middle)][1:]
-    todo.append((24.0, attended_end))
+    cache_load.wait()
+    todo = [(3.0 * n, step) for n, step in enumerate(middle)][1:]
+    todo.append((18.0, attended_end))
     for key in reversed(OUT.order):
         while todo and (OUT.end - OUT.times[key] > todo[0][0] or key[0][0] == "d"):
             todo.pop(0)[1]("d")
         scatter_node(key)
+
+    dec_sum = jnp.concatenate([oda[...], odb[...]], axis=1)
+    dsend2[:72] = jnp.where(yl == 0, dec_sum[72:], dec_sum[:72]).astype(BF16)
+    dsend2[72:] = jnp.zeros((8, TOK), BF16)
+    psend[...] = jnp.where(yl == 0, opb[...], opa[...]).astype(BF16)
+    start(psend, precv, fsend.at[0], frecv.at[0], partner)
+    start(dsend2, drecv2, fsend.at[1], frecv.at[1], partner)
+    arrive(precv, fsend.at[0], frecv.at[0])
+    pre_sum = jnp.where(yl == 0, opa[...], opb[...]) + precv[...].astype(F32)
+    for q in range(2):
+        pfin[q * BLK : q * BLK + BLK] = pre_sum[:, q * 128 : q * 128 + 128].astype(BF16)
+
+    @pl.when(turned)
+    def _():
+        remote(pfin, pland, fsend.at[2], frecv.at[2], keeper).start()
+
+    arrive(drecv2, fsend.at[1], frecv.at[1])
+    dec_sum = jnp.where(yl == 0, dec_sum[:72], dec_sum[72:]) + drecv2[:72].astype(F32)
+    for t in range(2):
+        decode_out[t] = dec_sum[:, t * 256 : t * 256 + 256].astype(BF16)
+
+    @pl.when(turned)
+    def _():
+        remote(pfin, pland, fsend.at[2], frecv.at[2], keeper).wait()
+        prefill_out[...] = pland[...]
+
+    @pl.when(x == gx)
+    def _():
+        prefill_out[...] = pfin[...]
+
+    for n, kind in enumerate(KINDS):
+        sent = got[kind].at[pl.ds(0, X * Z - 1)]
+        remote(sent, sent, send.at[n], recv.at[0], partner).wait_send()
+        sent = held[kind].at[pl.ds(0, X * Z - 1)]
+        remote(sent, sent, osend.at[n], orecv.at[0], partner).wait_send()
+    for o in range(2):
+        sent = winT.at[o, pl.ds(first, BLK)]
+        remote(sent, sent, esend.at[o], erecv.at[o], partner).wait_send()
     for c in pending:
         c.wait_send()
 
 
-def run(info, xpa, xpb, xda, xdb, wq, wkv, wt, cache):
+def run(info, dtok, wkv, ptok, wq, wo, cache):
     vmem = pl.BlockSpec(memory_space=pltpu.VMEM)
+    hbm = pl.BlockSpec(memory_space=pl.ANY)
     dma = pltpu.SemaphoreType.DMA
+    group = wq.shape[1]
+
+    def scratch(*shape, dtype=BF16):
+        return pltpu.VMEM(shape, dtype)
+
     return pl.pallas_call(
         kernel,
-        out_shape=tuple(jax.ShapeDtypeStruct((BLK, WIDTH[k]), F32) for k in KINDS),
-        in_specs=[pl.BlockSpec(memory_space=pltpu.SMEM)] + [vmem] * 8,
-        out_specs=(vmem,) * 4,
-        scratch_shapes=[pltpu.VMEM((X, Z * BLK, WIDTH[k]), BF16) for k in KINDS]
+        out_shape=(
+            jax.ShapeDtypeStruct((2 * BLK, PLEN), BF16),
+            jax.ShapeDtypeStruct((2, 72, 256), BF16),
+        ),
+        in_specs=[pl.BlockSpec(memory_space=pltpu.SMEM), vmem, vmem, hbm, hbm, hbm, hbm],
+        out_specs=(vmem, vmem),
+        scratch_shapes=[scratch(X * Z, BLK, WIDTH_IN[k]) for k in KINDS]
         + [
-            pltpu.VMEM((wq.shape[0], 256), BF16),
-            pltpu.VMEM((256, TOK), F32),
-            pltpu.VMEM((256, TOK), F32),
-            pltpu.VMEM((GX - 1, ROWS1, 128), F32),
-            pltpu.VMEM((GX - 1, ROWS1, 128), F32),
-            pltpu.VMEM((128, 256), F32),
-            pltpu.VMEM((4, X, Z, YL, 2, 256), F32),
-            pltpu.VMEM((4, X, Z, YL, 2, 256), F32),
-            pltpu.VMEM((4, X, Z, YL, 2, 256), F32),
-            pltpu.VMEM((4, 32, 256), F32),
-            pltpu.VMEM((96, 256), F32),
-            pltpu.VMEM((KVC, PLEN), F32),
-            pltpu.VMEM((Z, KVC, PLEN), F32),
-            pltpu.VMEM((X, Z, YL, KVC, PLEN), F32),
-            pltpu.VMEM((2, COLS, 128), BF16),
-            pltpu.VMEM((2, GX, COLS, 128), BF16),
-            pltpu.VMEM((COLS, TOK), BF16),
+            scratch(ROWS1, group),
+            scratch(COLS, group),
+            scratch(group, COLS),
+            scratch(*cache.shape),
+            scratch(2, PLEN, group),
+            scratch(2, PLEN, 256),
+            scratch(2, 256, PLEN),
         ]
-        + [pltpu.VMEM((X * Z, BLK, WIDTH[k]), BF16) for k in KINDS]
-        + [pltpu.VMEM((OUT.slots[k], BLK, WIDTH[k]), BF16) for k in KINDS]
+        + [scratch(BLK, WIDTH_IN[k]) for k in KINDS]
         + [
-            dma((NSEND,)),
+            scratch(80, TOK),
+            scratch(80, TOK),
+            scratch(ROWS1, TOK, dtype=F32),
+            scratch(ROWS1, TOK, dtype=F32),
+            scratch(GX - 1, ROWS1, 128, dtype=F32),
+            scratch(GX - 1, ROWS1, 128, dtype=F32),
+            scratch(128, 256, dtype=F32),
+            scratch(4, X, Z, YL, 2, 256, dtype=F32),
+            scratch(4, X, Z, YL, 2, 256, dtype=F32),
+            scratch(4, X, Z, YL, 2, 256, dtype=F32),
+            scratch(4, 32, 256, dtype=F32),
+            scratch(96, 256, dtype=F32),
+            scratch(KVC, PLEN, dtype=F32),
+            scratch(Z, KVC, PLEN, dtype=F32),
+            scratch(X, Z, YL, KVC, PLEN, dtype=F32),
+            scratch(2, COLS, 128),
+            scratch(2, GX, COLS, 128),
+            scratch(COLS, TOK),
+            scratch(COLS, TOK),
+        ]
+        + [scratch(X * Z, BLK, WIDTH_OUT[k]) for k in KINDS]
+        + [scratch(OUT.slots[k], BLK, WIDTH_OUT[k]) for k in KINDS]
+        + [scratch(BLK, WIDTH_OUT[k], dtype=F32) for k in KINDS]
+        + [
+            scratch(BLK, 256),
+            scratch(BLK, 256),
+            scratch(80, TOK),
+            scratch(80, TOK),
+            scratch(2 * BLK, PLEN),
+            scratch(2 * BLK, PLEN),
+            dma((8,)),
+            dma((4,)),
+            dma((4,)),
+            dma((4,)),
             dma((NSEND,)),
             dma((2, GX)),
             dma((2, GX)),
@@ -503,14 +675,16 @@
             dma((16,)),
             dma((2, GX)),
             dma((2, GX)),
+            dma((4,)),
             dma((NSEND,)),
-            dma((NSEND,)),
+            dma((4,)),
+            dma((4,)),
         ],
         compiler_params=pltpu.CompilerParams(
-            collective_id=0, has_side_effects=True, vmem_limit_bytes=58 * 2**20
+            collective_id=0, has_side_effects=True, vmem_limit_bytes=60 * 2**20
         ),
         name="attention_block",
-    )(info, xpa, xpb, xda, xdb, wq, wkv, wt, cache)
+    )(info, dtok, wkv, ptok, wq, wo, cache)
 
 
 def body(
@@ -523,48 +697,17 @@
     keyval_weight,
     out_weight,
 ):
-    gx, x, z, yl = place()
-    group = query_weight.shape[0]
-    slices = [
-        lax.dynamic_slice(prefill_tokens, (0, g * group + (x * Z + z) * BLK), (PLEN, BLK)).T
-        for g in range(GX)
-    ]
-    pre = lax.all_to_all(jnp.stack(slices), "gx", split_axis=0, concat_axis=0, tiled=True)
-    pre = pre.transpose(1, 0, 2).reshape(BLK, GX * PLEN)
-    dec = decode_tokens.reshape(2, GX, 64, 72).transpose(3, 1, 0, 2).reshape(72, 512)
-    other = lax.ppermute(dec, "yz", [(i, i ^ 1) for i in range(X * Z * YL)])
-    dec = jnp.where(
-        yl == 0, jnp.concatenate([dec, other], axis=0), jnp.concatenate([other, dec], axis=0)
-    )
-    split = WIDTH["pa"], WIDTH["da"]
     info = jnp.stack([cache_lengths[0], prefill_lengths[0]]).astype(jnp.int32)
-    opa, opb, oda, odb = run(
+    prefill_out, decode_out = run(
         info,
-        pre[:, : split[0]],
-        pre[:, split[0] :],
-        dec[:, : split[1]],
-        dec[:, split[1] :],
-        query_weight,
-        keyval_weight,
-        out_weight.T,
+        decode_tokens.transpose(0, 2, 1),
+        keyval_weight.T,
+        prefill_tokens,
+        query_weight.T,
+        out_weight,
         cache_keyvals[0],
     )
-
-    pre = jnp.concatenate([opa, opb], axis=1)
-    dec = jnp.concatenate([oda, odb], axis=1)
-    swap = [(i, i ^ 1) for i in range(X * Z * YL)]
-    dec_other = lax.ppermute(jnp.where(yl == 0, dec[72:], dec[:72]), "yz", swap)
-    pre_other = lax.ppermute(jnp.where(yl == 0, pre[:, 256:], pre[:, :256]), "yz", swap)
-    dec = jnp.where(yl == 0, dec[:72], dec[72:]) + dec_other
-    pre = jnp.where(yl == 0, pre[:, :256], pre[:, 256:]) + pre_other
-    decode_out = dec.reshape(72, GX, 2, 64).transpose(2, 1, 3, 0).reshape(2, 256, 72)
-    turn = []
-    for g in range(GX):
-        for i in range(X * Z * YL):
-            turn.append((g * 64 + i, (i // 16) * 64 + g * 16 + i % 16))
-    pre = lax.ppermute(pre.astype(BF16), ("gx", "yz"), turn)
-    prefill_out = pre.reshape(BLK, 2, PLEN).transpose(2, 1, 0).reshape(PLEN, 2 * BLK)
-    return (prefill_out, decode_out.astype(BF16))
+    return (prefill_out.T, decode_out.transpose(0, 2, 1))
 
 
 def solution(mesh):

time: 235 us -> 184 us (0.78)
  starting transfers between devices: 14.8 us -> 0 us
  Pallas kernels: 189 us -> 175 us
  local copies, waits for them, and re-layouts: 16.3 us -> 3.04 us
  waiting for transfers between devices: 6.13 us -> 0 us
  other arithmetic: 4.26 us -> 0.59 us
    pallas_call x1, Pallas kernels: 189 us -> 175 us  [run(): pl.pallas_call(kernel, out_shape=(jax.ShapeDtypeStruct((2 * BLK, PLEN), B...]
    ppermute x4 -> x0, starting transfers between devices: 10 us -> none  [the longest x1 6.55 us: body(): pre = lax.ppermute(pre.astype(BF16), ('gx', 'yz'), turn)]
    ppermute x4 -> x0, waiting for transfers between devices: 6.12 us -> none  [the longest x1 3.55 us: body(): lax.ppermute(jnp.where(yl == 0, pre[:, 256:], pre[:, :256]), 'yz', swap)]
    all_to_all x1 -> x0, starting transfers between devices: 4.8 us -> none  [body(): lax.all_to_all(jnp.stack(slices), 'gx', split_axis=0, concat_axis=0, tile...]
    unnamed x14 -> x2, local copies, waits for them, and re-layouts: 7.67 us -> 3.04 us
    reshape x4 -> x0, local copies, waits for them, and re-layouts: 2.87 us -> none  [the longest x2 1.93 us: body(): decode_tokens.reshape(2, GX, 64, 72).transpose(3, 1, 0, 2).reshape(72, 512)]
  transfers between devices with their start and end apart: 5 -> 0, of which waited for: 2 -> 0; matrix products, arithmetic and copies ran while one was open for 6% -> 0% of each run, Pallas kernels for 0% -> 0%
where the time goes in v3:
time: 184 us; the launch traced here: 181 us
  Pallas kernels  175 us (95%)
  local copies, waits for them, and re-layouts  3.04 us (2%)
  between operations  1.93 us (1%)
    pallas_call x1, Pallas kernels, run(): pl.pallas_call(kernel, out_shape=(jax.ShapeDtypeStruct((2 * BLK, PLEN), B...  175 us

profile of v3, /device:TPU:16, one launch (start us, length us, event | category | flops | bytes accessed | tf_op | source)
XLA Modules:
  0.0 180.7 jit_solution(15943807099857114110)
XLA Ops:
  1.9 0.6 pad_add_fusion.info
  2.5 175.2 %attention_block.1 = (bf16[288,128]{1,0:T(8,128)(2,1)}, bf16[2,72,256]{2,1,0:T(8,128)(2,1)}) custom-call(s32[2]{0:T(128)} %pad_add_fusion.info, bf16[2,72,256]{2,1,0:T(8,128)(2,1)} %bitcast.10, bf16[8,4608]{1,0:T(8,128)(2,1)} %bitcast.11, bf16[128,18432]{1,0:T(8,128)(2,1)} %ptok.1, bf16[192,4608]{1,0:T(8,128)(2,1)} %bitcast.7, bf16[192,4608]{1,0:T(8,128)(2,1)} %wo.1, ...), custom_call_target="tpu_custom_call" | custom-call | tf_op jit(solution)/shard_map/attention_block/pallas_call | solution.py:615
  177.7 1.5 copy.14
  179.2 1.5 copy.15

commit v4 on v3

v4 whole, which is shorter than its diff:
```python
import heapq

import jax
import jax.numpy as jnp
from jax import lax
from jax.experimental import pallas as pl
from jax.experimental.pallas import tpu as pltpu
from jax.sharding import PartitionSpec as P

HEADS = 48
HD = 256
PLEN = 128
GX, X, Z, YL = 4, 4, 8, 2
BLK = 144
TOK = 512
WIDTH_IN = {"p0": 1024, "p1": 1024, "da": 128, "db": 384}
WIDTH_OUT = {"pa": 256, "pb": 256, "da": 384, "db": 128}
START_IN = {"da": 0, "db": 128}
START = {"pa": 0, "pb": 256, "da": 0, "db": 384}
KINDS = tuple(START)
KINDS_IN = tuple(WIDTH_IN)
SPAN = Z * BLK
COLS = 192
KVC = 8
ROWS1 = 208
MESH = pl.DeviceIdType.MESH
F32 = jnp.float32
BF16 = jnp.bfloat16
FULL, UPPER, LOWER = (0, 144), (0, 80), (80, 64)
OPPOSITE = {"x+": "x-", "x-": "x+", "z+": "z-", "z-": "z+"}


def steps_from(key):
    kind, xo, zo = key
    out = []
    if kind in ("p0", "p1"):
        if xo == 0:
            out.append(("x+", FULL, (kind, -1, 0)))
            out.append(("x-", FULL, (kind, 1, 0)))
        elif kind == "p0" and xo == -1:
            out.append(("x+", FULL, (kind, 2, 0)))
        elif kind == "p1" and xo == 1:
            out.append(("x-", FULL, (kind, 2, 0)))
    elif kind[1] == "a":
        if xo == 0:
            if -3 < zo <= 0:
                out.append(("z+", FULL, (kind, 0, zo - 1)))
            if zo == -3:
                out.append(("z+", UPPER, (kind, 0, 4)))
            if 0 <= zo < 3:
                out.append(("z-", FULL, (kind, 0, zo + 1)))
            if zo == 3:
                out.append(("z-", LOWER, (kind, 0, 4)))
            out.append(("x+", FULL, (kind, -1, zo)))
            out.append(("x-", FULL, (kind, 1, zo)))
        elif xo == -1 and zo % 2 == 0:
            out.append(("x+", FULL, (kind, 2, zo)))
        elif xo == 1 and zo % 2 == 1:
            out.append(("x-", FULL, (kind, 2, zo)))
    else:
        if zo == 0:
            if xo == 0:
                out.append(("x+", FULL, (kind, -1, 0)))
                out.append(("x-", FULL, (kind, 1, 0)))
            elif xo == -1:
                out.append(("x+", UPPER, (kind, 2, 0)))
            elif xo == 1:
                out.append(("x-", LOWER, (kind, 2, 0)))
        if zo <= 0 and (zo > -3 or xo in (0, 2)):
            out.append(("z+", FULL, (kind, xo, zo - 1 if zo > -3 else 4)))
        if 0 <= zo <= 3 and (zo < 3 or xo in (-1, 1)):
            out.append(("z-", FULL, (kind, xo, zo + 1)))
    return out


class Plan:
    def __init__(self, releases, width):
        free = dict.fromkeys(OPPOSITE, 0.0)
        events, self.order, self.times, self.pieces = [], [], {}, {}
        self.sends, self.fills, self.source, self.where = {}, {}, {}, {}
        self.slots = dict.fromkeys(releases, 0)

        def leave(key, now):
            self.order.append(key)
            self.times[key] = now
            for n, (d, rows, there) in enumerate(steps_from(key)):
                free[d] = max(free[d], now) + width[key[0]] * rows[1] * 4e-5
                k = len(self.sends)
                self.sends[(key, n)] = k
                self.fills[(there, rows)] = k
                self.source[k] = (key, n)
                self.where[(key, n)] = self.slots[key[0]]
                self.slots[key[0]] += 1
                heapq.heappush(events, (free[d] + 3.0, k, there, (d, rows)))

        for n, kind in enumerate(releases):
            heapq.heappush(events, (releases[kind], n - len(releases), (kind, 0, 0), None))
        while events:
            now, _, key, piece = heapq.heappop(events)
            if piece is not None:
                self.pieces.setdefault(key, []).append(piece)
            if piece is None or sum(p[1][1] for p in self.pieces[key]) == BLK:
                leave(key, now)
        self.end = max(self.times.values())


IN = Plan({"db": 0.0, "da": 0.0, "p0": 6.0, "p1": 12.0}, WIDTH_IN)
OUT = Plan({"db": 0.0, "da": 0.0, "pb": 10.0, "pa": 10.0}, WIDTH_OUT)
MIDDLE = (0.0, 4.5, 12.0, 21.5, 26.0)


def place():
    gx = lax.axis_index("gx")
    yz = lax.axis_index("yz")
    return gx, yz // (Z * YL), (yz // YL) % Z, yz % YL


def flat(x, z, yl):
    return x * (Z * YL) + z * YL + yl


def copy_rows(move):
    def four(g, carry):
        for j in range(4):
            move(4 * g + j, g, j)
        return carry

    lax.fori_loop(0, 16, four, 0)


def kernel(
    cache_length, prefill_length, dtok, wkv, ptok, wq, wo, cache_hbm,
    prefill_out, decode_out,
    gp0, gp1, gda, gdb, w, wov, wt, cache, tloc, xda, xdb, dsend, drecv,
    accp, accd, give, takep, taked, tok, s1, r2, qj, qh,
    kvown, k2, att, heads, dec, dec2, ppa, ppb, pda, pdb, lpa, lpb, lda, ldb,
    opa, opb, oda, odb, psend, precv, dsend2, drecv2, pfin, pland,
    local, esend, erecv, send, recv, gsend, grecv, asend, arecv, hsend, hrecv,
    osend, orecv, fsend, frecv,
):
    gx, x, z, yl = place()
    yz = lax.axis_index("yz")
    core, y_hi = gx % 2, gx // 2
    own = {"da": xda, "db": xdb}
    got = dict(zip(KINDS_IN, (gp0, gp1, gda, gdb)))
    result = dict(zip(KINDS, (opa, opb, oda, odb)))
    held = dict(zip(KINDS, (ppa, ppb, pda, pdb)))
    landing = dict(zip(KINDS, (lpa, lpb, lda, ldb)))
    acc = {"p": accp, "d": accd}
    take = {"p": takep, "d": taked}
    pending = []

    def near(d):
        dx = {"x+": 1, "x-": X - 1}.get(d, 0)
        dz = {"z+": 1, "z-": Z - 1}.get(d, 0)
        return (gx, flat((x + dx) % X, (z + dz) % Z, yl))

    g_peers = [((gx + s) % GX, yz) for s in range(1, GX)]
    there = 1 - y_hi
    across = [(2 * there + o, flat(x, z, 1 - yl)) for o in range(2)]
    many = X * Z * YL

    def remote(src, dst, ssem, rsem, device):
        return pltpu.make_async_remote_copy(
            src_ref=src, dst_ref=dst, send_sem=ssem, recv_sem=rsem, device_id=device, device_id_type=MESH
        )

    def start(src, dst, ssem, rsem, device):
        c = remote(src, dst, ssem, rsem, device)
        c.start()
        pending.append(c)

    def arrive(dst, ssem, rsem):
        remote(dst, dst, ssem, rsem, near("x+")).wait_recv()

    barrier = pltpu.get_barrier_semaphore()
    peers = g_peers + across
    keeper = (x, flat(gx, z, yl))
    turned = x != gx

    def greet(n, carry):
        pl.semaphore_signal(barrier, inc=1, device_id=(gx, (yz + n) % many), device_id_type=MESH)
        return carry

    lax.fori_loop(1, many, greet, 0)
    for peer in peers:
        pl.semaphore_signal(barrier, inc=1, device_id=peer, device_id_type=MESH)

    @pl.when(turned)
    def _():
        pl.semaphore_signal(barrier, inc=1, device_id=keeper, device_id_type=MESH)

    group = wq.shape[1]
    loads = []

    def load(src, dst):
        c = pltpu.make_async_copy(src, dst, local.at[len(loads)])
        c.start()
        loads.append(c)
        return c

    dsend[:72, :256] = dtok[0]
    dsend[:72, 256:] = dtok[1]
    dsend[72:, :] = jnp.zeros((8, TOK), BF16)
    pl.semaphore_wait(barrier, many - 1 + len(peers) + turned.astype(jnp.int32))

    partner = (gx, flat(x, z, 1 - yl))
    start(dsend, drecv, esend.at[2], erecv.at[2], partner)
    for c in range(2):

        @pl.when(core == c)
        def _(c=c):
            for o in range(2):
                lane = pl.multiple_of((2 * there + o) * group + x * SPAN, 128)
                remote(
                    ptok.at[:, pl.ds(lane, SPAN)],
                    got["p%d" % c].at[x],
                    esend.at[o],
                    erecv.at[c],
                    across[o],
                ).start()

    w_load = load(wq, w.at[pl.ds(0, COLS)])
    mine_load = load(ptok.at[:, pl.ds(pl.multiple_of(gx * group, 128), group)], tloc.at[0])
    sibling_gx = gx + 1 - 2 * core
    start(
        ptok.at[:, pl.ds(pl.multiple_of(sibling_gx * group, 128), group)],
        tloc.at[1],
        esend.at[3],
        erecv.at[3],
        (sibling_gx, yz),
    )
    wo_load = load(wo, wov)
    cache_load = load(cache_hbm, cache)
    tok[...] = jnp.zeros(tok.shape, F32)
    qj[...] = jnp.zeros(qj.shape, F32)

    def slot(key, rows):
        kind, xo, zo = key
        if kind[0] == "p":
            return got[kind].at[(x + xo) % X]
        return got[kind].at[((x + xo) % X) * Z + (z + zo) % Z, pl.ds(rows[0], rows[1])]

    seen = {}

    def multiply(kind, xo):
        xx = (x + xo) % X
        part_of_w = w[:, pl.ds(pl.multiple_of(xx * SPAN, 128), SPAN)]
        if kind[0] == "p":
            part = lax.dot_general(
                part_of_w, got[kind][xx], (((1,), (1,)), ((), ())), preferred_element_type=F32
            )
            lanes = pl.ds(pl.multiple_of((2 * there + int(kind[1])) * 128, 128), 128)
        else:
            block = got[kind][pl.ds(xx * Z, Z)].reshape(SPAN, WIDTH_IN[kind])
            part = jnp.dot(part_of_w, block, preferred_element_type=F32)
            lanes = slice(START_IN[kind], START_IN[kind] + WIDTH_IN[kind])
        if kind in seen:
            acc[kind[0]][:, lanes] += part
        else:
            acc[kind[0]][:, lanes] = part
            seen[kind] = True

    def multiply_near(n):
        lanes = pl.ds(pl.multiple_of((gx if n == 0 else sibling_gx) * 128, 128), 128)
        acc["p"][:, lanes] = lax.dot_general(
            w[...], tloc[n], (((1,), (1,)), ((), ())), preferred_element_type=F32
        )

    def gather_node(key):
        kind, xo, zo = key
        mine = (xo, zo) == (0, 0)
        if not mine:
            for _, rows in IN.pieces[key]:
                k = IN.fills[(key, rows)]
                arrive(slot(key, rows), send.at[KINDS_IN.index(kind)], recv.at[k])
        elif kind[0] == "p":
            c = int(kind[1])
            arrive(slot(key, FULL), esend.at[c], erecv.at[c])
        elif kind == "db":
            arrive(drecv, esend.at[2], erecv.at[2])
            one, two = dsend[:72].astype(F32), drecv[:72].astype(F32)
            both = jnp.where(
                yl == 0, jnp.concatenate([one, two], axis=0), jnp.concatenate([two, one], axis=0)
            ).astype(BF16)
            xda[...] = both[:, : WIDTH_IN["da"]]
            xdb[...] = both[:, WIDTH_IN["da"] :]
        for n, (d, rows, there) in enumerate(steps_from(key)):
            k = IN.sends[(key, n)]
            remote(
                own[kind] if mine and kind in own else slot(key, rows),
                slot(key, rows),
                send.at[KINDS_IN.index(kind)],
                recv.at[k],
                near(d),
            ).start()
        if mine and kind in own:
            got[kind][x * Z + z] = own[kind][...]
        seen[(kind, xo)] = seen.get((kind, xo), 0) + 1
        if seen[(kind, xo)] == (1 if kind[0] == "p" else Z):
            multiply(kind, xo)

    def sum_start(f):
        if f == "d":
            rows = accd[...]
            for g in range(GX):
                accd[:, g * 128 : g * 128 + 64] = rows[:, g * 64 : g * 64 + 64]
                accd[:, g * 128 + 64 : g * 128 + 128] = rows[:, 256 + g * 64 : 320 + g * 64]
        for g in range(GX):
            give[n_of[f], g] = acc[f][:, g * 128 : g * 128 + 128].astype(BF16)
        for s in range(1, GX):
            start(
                give.at[n_of[f], (gx + s) % GX],
                take[f].at[s - 1],
                gsend.at[n_of[f], s],
                grecv.at[n_of[f], s],
                g_peers[s - 1],
            )

    n_of = {"p": 0, "d": 1}

    def exchange_start(i, also=None):
        def one(n, carry):
            to = (yz + n) % many
            remote(s1.at[i, to], r2.at[i, yz], asend.at[i], arecv.at[i], (gx, to)).start()
            if also:
                remote(kvown, k2.at[yz], asend.at[4], arecv.at[4], (gx, to)).start()
            return carry

        lax.fori_loop(1, many, one, 0)
        r2[i, yz] = s1[i, yz]
        if also:
            k2[yz] = kvown[...]

    def exchange_end(i):
        arrive(r2.at[i, pl.ds(0, many - 1)], asend.at[i], arecv.at[i])

    def token(f, r, t):
        return 2 * r + t if f == "p" else t * 64 + r

    def queries_start(f):
        for s in range(1, GX):
            arrive(take[f].at[s - 1], gsend.at[n_of[f], s], grecv.at[n_of[f], s])
        lane = pl.multiple_of(gx * 128, 128)
        total = acc[f][:, pl.ds(lane, 128)]
        for s in range(1, GX):
            total = total + take[f][s - 1].astype(F32)
        total = total.astype(BF16).astype(F32)
        tok[:, :ROWS1] = total.T
        i = 2 * n_of[f]

        def pack(r, g, j):
            for t in range(2):
                s1[i, r, pl.ds(t, 1), :] = tok[pl.ds(token(f, r, t), 1), :]

        copy_rows(pack)
        if f == "p":
            kvown[...] = total[COLS : COLS + KVC]
        exchange_start(i, f == "p")

    nt = (((1,), (1,)), ((), ()))
    scale = HD ** (-0.5)

    def attend(f):
        i = 2 * n_of[f]
        exchange_end(i)

        def unpack(r, g, j):
            for t in range(2):
                qj[j, pl.ds(t * 16 + g, 1), :] = r2[i, r, pl.ds(t, 1), :]

        copy_rows(unpack)
        qh[0:32, :192] = qj[0, :, :192]
        qh[0:32, 192:] = qj[1, :, :64]
        qh[32:64, :128] = qj[1, :, 64:192]
        qh[32:64, 128:] = qj[2, :, :128]
        qh[64:96, :64] = qj[2, :, 128:192]
        qh[64:96, 64:] = qj[3, :, :192]
        q32 = qh[...]
        q = q32.astype(BF16)
        if f == "p":
            arrive(k2.at[pl.ds(0, many - 1)], asend.at[4], arecv.at[4])
            kvt = k2[...].reshape(2 * HD, PLEN).astype(BF16)
            s = jnp.dot(q, kvt[:HD], preferred_element_type=F32) * scale
            query = 2 * yz + (lax.broadcasted_iota(jnp.int32, s.shape, 0) // 16) % 2
            pos = lax.broadcasted_iota(jnp.int32, s.shape, 1)
            s = jnp.where((pos <= query) & (pos < prefill_length[0]), s, -1e30)
            e = jnp.exp(s - jnp.max(s, axis=1, keepdims=True))
            probs = (e / jnp.sum(e, axis=1, keepdims=True)).astype(BF16)
            out = lax.dot_general(probs, kvt[HD:], nt, preferred_element_type=F32)
        else:
            row = lax.broadcasted_iota(jnp.int32, (KVC, 2 * HD), 0)
            lane = lax.broadcasted_iota(jnp.int32, (KVC, 2 * HD), 1)
            spread = (lane % KVC == row).astype(BF16)
            group = lax.broadcasted_iota(jnp.int32, (32, 2 * HD), 0) % 16
            holder = lax.broadcasted_iota(jnp.int32, (32, 2 * HD), 1) // KVC
            new = jnp.zeros((32, 2 * HD), F32)
            for j in range(4):
                wide = jnp.dot(
                    qj[j, :, COLS : COLS + KVC].astype(BF16), spread, preferred_element_type=F32
                )
                new = new + jnp.where(holder == 4 * group + j, wide, 0.0)
            new0 = jnp.sum(new[:16], axis=0, keepdims=True)
            new1 = jnp.sum(new[16:], axis=0, keepdims=True)
            s = lax.dot_general(q, cache[:, :HD], nt, preferred_element_type=F32) * scale
            pos = lax.broadcasted_iota(jnp.int32, s.shape, 1)
            s = jnp.where(pos < cache_length[0], s, -1e30)
            f0 = jnp.sum(q32 * new0[:, :HD], axis=1, keepdims=True) * scale
            f1 = jnp.sum(q32 * new1[:, :HD], axis=1, keepdims=True) * scale
            step = (lax.broadcasted_iota(jnp.int32, f1.shape, 0) // 16) % 2
            f1 = jnp.where(step == 1, f1, -1e30)
            peak = jnp.maximum(jnp.max(s, axis=1, keepdims=True), jnp.maximum(f0, f1))
            es, e0, e1 = jnp.exp(s - peak), jnp.exp(f0 - peak), jnp.exp(f1 - peak)
            total = jnp.sum(es, axis=1, keepdims=True) + e0 + e1
            out = jnp.dot((es / total).astype(BF16), cache[:, HD:], preferred_element_type=F32)
            out = out + (e0 / total).astype(BF16).astype(F32) * new0[:, HD:]
            out = out + (e1 / total).astype(BF16).astype(F32) * new1[:, HD:]
        qh[...] = out.astype(BF16).astype(F32)
        qj[0, :, :192] = qh[0:32, :192]
        qj[1, :, :64] = qh[0:32, 192:]
        qj[1, :, 64:192] = qh[32:64, :128]
        qj[2, :, :128] = qh[32:64, 128:]
        qj[2, :, 128:192] = qh[64:96, :64]
        qj[3, :, :192] = qh[64:96, 64:]

        def pack(r, g, j):
            for t in range(2):
                s1[i + 1, r, pl.ds(t, 1), :] = qj[j, pl.ds(t * 16 + g, 1), :]

        copy_rows(pack)
        exchange_start(i + 1)

    def attended_share(f):
        n = n_of[f]
        i = 2 * n + 1
        exchange_end(i)

        def unpack(r, g, j):
            for t in range(2):
                tok[pl.ds(token(f, r, t), 1), :] = r2[i, r, pl.ds(t, 1), :]

        copy_rows(unpack)
        att[n] = tok[...].T[:COLS].astype(BF16)
        for s in range(1, GX):
            start(att.at[n], heads.at[n, s], hsend.at[n, s], hrecv.at[n, s], g_peers[s - 1])
        heads[n, 0] = att[n]

    def attended_end(f):
        n = n_of[f]
        for s in range(1, GX):
            arrive(heads.at[n, s], hsend.at[n, s], hrecv.at[n, s])
        if f == "d":
            for s in range(GX):
                lane = pl.multiple_of(((gx - s + GX) % GX) * 128, 128)
                dec2[:, pl.ds(lane, 128)] = heads[n, s]
            for g in range(GX):
                for t in range(2):
                    dec[:, t * 256 + g * 64 : t * 256 + g * 64 + 64] = dec2[
                        :, g * 128 + t * 64 : g * 128 + t * 64 + 64
                    ]

    def terms(key):
        kind, xo, zo = key
        xx, zz = (x + xo) % X, (z + zo) % Z
        if kind[0] == "d":
            first = pl.multiple_of((xx * Z + zz) * BLK, 16)
            lanes = slice(START[kind], START[kind] + WIDTH_OUT[kind])
            return jnp.dot(wt[pl.ds(first, BLK), :], dec[:, lanes], preferred_element_type=F32)
        group = heads[0, (gx - xx + GX) % GX]
        parts = []
        for q in range(START[kind] // 128, (START[kind] + WIDTH_OUT[kind]) // 128):
            first = pl.multiple_of(zz * (4 * BLK) + q * BLK, 16)
            parts.append(jnp.dot(wt[pl.ds(first, BLK), :], group, preferred_element_type=F32))
        return jnp.concatenate(parts, axis=1)

    def scatter_node(key):
        kind, xo, zo = key
        last = (xo, zo) == (0, 0)
        at = ((x + xo) % X) * Z + (z + zo) % Z
        local = terms(key)
        steps = steps_from(key)
        for n, (d, rows, there) in enumerate(steps):
            k = OUT.sends[(key, n)]
            spot = landing[kind].at[OUT.where[(key, n)], pl.ds(rows[0], rows[1])]
            arrive(spot, osend.at[KINDS.index(kind)], orecv.at[k])
        halves = [local[:80], local[80:]]
        for n, (d, rows, there) in enumerate(steps):
            for i, (r0, rn) in enumerate((UPPER, LOWER)):
                if rows[0] <= r0 and r0 + rn <= rows[0] + rows[1]:
                    halves[i] = halves[i] + landing[kind][OUT.where[(key, n)], r0 : r0 + rn].astype(F32)
        for i, (r0, rn) in enumerate((UPPER, LOWER)):
            if last:
                result[kind][r0 : r0 + rn] = halves[i]
            else:
                held[kind][at, r0 : r0 + rn] = halves[i].astype(BF16)
        if not last:
            for d, rows in OUT.pieces[key]:
                k = OUT.fills[(key, rows)]
                remote(
                    held[kind].at[at, pl.ds(rows[0], rows[1])],
                    landing[kind].at[OUT.where[OUT.source[k]], pl.ds(rows[0], rows[1])],
                    osend.at[KINDS.index(kind)],
                    orecv.at[k],
                    near(OPPOSITE[d]),
                ).start()

    def prefill_halves():
        psend[...] = jnp.where(yl == 0, opb[...], opa[...]).astype(BF16)
        start(psend, precv, fsend.at[0], frecv.at[0], partner)

    def prefill_turn():
        arrive(precv, fsend.at[0], frecv.at[0])
        pre_sum = jnp.where(yl == 0, opa[...], opb[...]) + precv[...].astype(F32)
        for q in range(2):
            pfin[q * BLK : q * BLK + BLK] = pre_sum[:, q * 128 : q * 128 + 128].astype(BF16)

        @pl.when(turned)
        def _():
            remote(pfin, pland, fsend.at[2], frecv.at[2], keeper).start()

    def prefill_end():
        @pl.when(turned)
        def _():
            remote(pfin, pland, fsend.at[2], frecv.at[2], keeper).wait()
            prefill_out[...] = pland[...]

        @pl.when(x == gx)
        def _():
            prefill_out[...] = pfin[...]

    def weights():
        w_load.wait()
        w[COLS:, :] = jnp.concatenate([wkv[...].astype(F32), jnp.zeros((8, group), F32)]).astype(BF16)
        mine_load.wait()
        multiply_near(0)

    def turn_weights():
        wo_load.wait()
        for n in range(group // 512):
            wt[pl.ds(512 * n, 512), :] = wov[:, 512 * n : 512 * n + 512].T

    def sibling():
        arrive(tloc.at[1], esend.at[3], erecv.at[3])
        multiply_near(1)
        cache_load.wait()

    middle = (sum_start, queries_start, attend, attended_share, attended_end)
    todo = [(IN.times[key], gather_node, key) for key in IN.order]
    todo.append((1.5, lambda _: weights(), None))
    todo.append((9.0, lambda _: sibling(), None))
    ends = {}
    for f in "pd":
        ready = max(IN.times[key] for key in IN.order if key[0][0] == f) + 0.5
        todo += [(ready + MIDDLE[n], step, f) for n, step in enumerate(middle)]
        ends[f] = ready + MIDDLE[-1]
        if f == "p":
            todo.append((ready + MIDDLE[1] + 0.1, lambda _: turn_weights(), None))
    begin = ends["p"] + 0.1
    out_times = {key: begin + OUT.end - OUT.times[key] for key in OUT.order}
    first_d = min(t for key, t in out_times.items() if key[0][0] == "d")
    shift = max(0.0, ends["d"] + 0.1 - first_d)
    for key in reversed(OUT.order):
        todo.append((out_times[key] + (shift if key[0][0] == "d" else 0.0), scatter_node, key))
    last_p = max(t for key, t in out_times.items() if key[0][0] == "p")
    todo.append((last_p + 0.1, lambda _: prefill_halves(), None))
    todo.append((last_p + 6.0, lambda _: prefill_turn(), None))
    for _, step, what in sorted(todo, key=lambda entry: entry[0]):
        step(what)

    dec_sum = jnp.concatenate([oda[...], odb[...]], axis=1)
    dsend2[:72] = jnp.where(yl == 0, dec_sum[72:], dec_sum[:72]).astype(BF16)
    dsend2[72:] = jnp.zeros((8, TOK), BF16)
    start(dsend2, drecv2, fsend.at[1], frecv.at[1], partner)
    prefill_end()
    arrive(drecv2, fsend.at[1], frecv.at[1])
    dec_sum = jnp.where(yl == 0, dec_sum[:72], dec_sum[72:]) + drecv2[:72].astype(F32)
    for t in range(2):
        decode_out[t] = dec_sum[:, t * 256 : t * 256 + 256].astype(BF16)

    for n, kind in enumerate(KINDS_IN):
        sent = got[kind].at[pl.ds(0, 3 if kind[0] == "p" else X * Z - 1)]
        remote(sent, sent, send.at[n], recv.at[0], partner).wait_send()
    for n, kind in enumerate(KINDS):
        sent = held[kind].at[pl.ds(0, X * Z - 1)]
        remote(sent, sent, osend.at[n], orecv.at[0], partner).wait_send()
    for o in range(2):
        sent = got["p0"].at[0]
        remote(sent, sent, esend.at[o], erecv.at[o], partner).wait_send()
    for i in range(4):
        sent = s1.at[i, pl.ds(0, many - 1)]
        remote(sent, sent, asend.at[i], arecv.at[i], partner).wait_send()
    sent = k2.at[pl.ds(0, many - 1)]
    remote(sent, sent, asend.at[4], arecv.at[4], partner).wait_send()
    for c in pending:
        c.wait_send()


def run(cache_length, prefill_length, dtok, wkv, ptok, wq, wo, cache):
    vmem = pl.BlockSpec(memory_space=pltpu.VMEM)
    hbm = pl.BlockSpec(memory_space=pl.ANY)
    dma = pltpu.SemaphoreType.DMA
    group = wq.shape[1]

    def scratch(*shape, dtype=BF16):
        return pltpu.VMEM(shape, dtype)

    return pl.pallas_call(
        kernel,
        out_shape=(
            jax.ShapeDtypeStruct((2 * BLK, PLEN), BF16),
            jax.ShapeDtypeStruct((2, 72, 256), BF16),
        ),
        in_specs=[pl.BlockSpec(memory_space=pltpu.SMEM)] * 2 + [vmem, vmem, hbm, hbm, hbm, hbm],
        out_specs=(vmem, vmem),
        scratch_shapes=[
            scratch(X, PLEN, SPAN),
            scratch(X, PLEN, SPAN),
            scratch(X * Z, BLK, WIDTH_IN["da"]),
            scratch(X * Z, BLK, WIDTH_IN["db"]),
            scratch(ROWS1, group),
            scratch(COLS, group),
            scratch(group, COLS),
            scratch(*cache.shape),
            scratch(2, PLEN, group),
            scratch(BLK, WIDTH_IN["da"]),
            scratch(BLK, WIDTH_IN["db"]),
            scratch(80, TOK),
            scratch(80, TOK),
            scratch(ROWS1, TOK, dtype=F32),
            scratch(ROWS1, TOK, dtype=F32),
            scratch(2, GX, ROWS1, 128),
            scratch(GX - 1, ROWS1, 128),
            scratch(GX - 1, ROWS1, 128),
            scratch(128, 256, dtype=F32),
            scratch(4, X * Z * YL, 2, 256, dtype=F32),
            scratch(4, X * Z * YL, 2, 256, dtype=F32),
            scratch(4, 32, 256, dtype=F32),
            scratch(96, 256, dtype=F32),
            scratch(KVC, PLEN, dtype=F32),
            scratch(X * Z * YL, KVC, PLEN, dtype=F32),
            scratch(2, COLS, 128),
            scratch(2, GX, COLS, 128),
            scratch(COLS, TOK),
            scratch(COLS, TOK),
        ]
        + [scratch(X * Z, BLK, WIDTH_OUT[k]) for k in KINDS]
        + [scratch(OUT.slots[k], BLK, WIDTH_OUT[k]) for k in KINDS]
        + [scratch(BLK, WIDTH_OUT[k], dtype=F32) for k in KINDS]
        + [
            scratch(BLK, 256),
            scratch(BLK, 256),
            scratch(80, TOK),
            scratch(80, TOK),
            scratch(2 * BLK, PLEN),
            scratch(2 * BLK, PLEN),
            dma((4,)),
            dma((4,)),
            dma((4,)),
            dma((4,)),
            dma((len(IN.sends),)),
            dma((2, GX)),
            dma((2, GX)),
            dma((5,)),
            dma((5,)),
            dma((2, GX)),
            dma((2, GX)),
            dma((4,)),
            dma((len(OUT.sends),)),
            dma((3,)),
            dma((3,)),
        ],
        compiler_params=pltpu.CompilerParams(
            collective_id=0, has_side_effects=True, vmem_limit_bytes=60 * 2**20
        ),
        name="attention_block",
    )(cache_length, prefill_length, dtok, wkv, ptok, wq, wo, cache)


def body(
    prefill_tokens,
    prefill_lengths,
    decode_tokens,
    cache_lengths,
    cache_keyvals,
    query_weight,
    keyval_weight,
    out_weight,
):
    prefill_out, decode_out = run(
        cache_lengths,
        prefill_lengths,
        decode_tokens.transpose(0, 2, 1),
        keyval_weight.T,
        prefill_tokens,
        query_weight.T,
        out_weight,
        cache_keyvals[0],
    )
    return (prefill_out.T, decode_out.transpose(0, 2, 1))


def solution(mesh):
    in_specs = (
        P("gx", None),
        P("gx"),
        P(None, None, ("gx", "yz")),
        P(("gx", "yz")),
        P(("gx", "yz"), None, None),
        P("gx", "yz"),
        P("gx", "yz"),
        P("yz", "gx"),
    )
    out_specs = (P("gx", "yz"), P(None, None, ("gx", "yz")))
    return jax.shard_map(body, mesh=mesh, in_specs=in_specs, out_specs=out_specs, check_vma=False)
```

time: 184 us -> 157 us (0.85); the launches traced: 181 us -> 156 us
  Pallas kernels: 175 us -> 151 us
    pallas_call x1, Pallas kernels: 175 us -> 151 us  [run(): pl.pallas_call(kernel, out_shape=(jax.ShapeDtypeStruct((2 * BLK, PLEN), B...]
where the time goes in v4:
time: 157 us; the launch traced here: 156 us
  Pallas kernels  151 us (96%)
  local copies, waits for them, and re-layouts  3.04 us (2%)
  between operations  1.93 us (1%)
    pallas_call x1, Pallas kernels, run(): pl.pallas_call(kernel, out_shape=(jax.ShapeDtypeStruct((2 * BLK, PLEN), B...  151 us

profile of v4, /device:TPU:16, one launch (start us, length us, event | category | flops | bytes accessed | tf_op | source)
XLA Modules:
  0.0 155.8 jit_solution(16793865233805873439)
XLA Ops:
  1.9 150.9 %attention_block.1 = (bf16[288,128]{1,0:T(8,128)(2,1)}, bf16[2,72,256]{2,1,0:T(8,128)(2,1)}) custom-call(s32[1]{0:T(128)S(6)} %copy.13.cache_length, s32[1]{0:T(128)S(6)} %copy.12.prefill_length, bf16[2,72,256]{2,1,0:T(8,128)(2,1)} %bitcast.10, bf16[8,4608]{1,0:T(8,128)(2,1)} %bitcast.11, bf16[128,18432]{1,0:T(8,128)(2,1)} %ptok.1, ...), custom_call_target="tpu_custom_call" | custom-call | tf_op jit(solution)/shard_map/attention_block/pallas_call | solution.py:607
  152.8 1.5 copy.14
  154.3 1.5 copy.15

commit v5 on v4

--- a/solution.py
+++ b/solution.py
@@ -19,6 +19,7 @@
 START = {"pa": 0, "pb": 256, "da": 0, "db": 384}
 KINDS = tuple(START)
 KINDS_IN = tuple(WIDTH_IN)
+FAR = {"p0": 21.0, "p1": 27.0}
 SPAN = Z * BLK
 COLS = 192
 KVC = 8
@@ -37,10 +38,6 @@
         if xo == 0:
             out.append(("x+", FULL, (kind, -1, 0)))
             out.append(("x-", FULL, (kind, 1, 0)))
-        elif kind == "p0" and xo == -1:
-            out.append(("x+", FULL, (kind, 2, 0)))
-        elif kind == "p1" and xo == 1:
-            out.append(("x-", FULL, (kind, 2, 0)))
     elif kind[1] == "a":
         if xo == 0:
             if -3 < zo <= 0:
@@ -95,6 +92,8 @@
 
         for n, kind in enumerate(releases):
             heapq.heappush(events, (releases[kind], n - len(releases), (kind, 0, 0), None))
+            if kind in FAR:
+                heapq.heappush(events, (FAR[kind], n - len(releases), (kind, 2, 0), None))
         while events:
             now, _, key, piece = heapq.heappop(events)
             if piece is not None:
@@ -104,9 +103,10 @@
         self.end = max(self.times.values())
 
 
-IN = Plan({"db": 0.0, "da": 0.0, "p0": 6.0, "p1": 12.0}, WIDTH_IN)
-OUT = Plan({"db": 0.0, "da": 0.0, "pb": 10.0, "pa": 10.0}, WIDTH_OUT)
-MIDDLE = (0.0, 4.5, 12.0, 21.5, 26.0)
+IN = Plan({"db": 0.0, "da": 0.0, "p0": 9.0, "p1": 15.0}, WIDTH_IN)
+OUT = Plan({"db": 0.0, "da": 0.0, "pb": 20.0, "pa": 20.0}, WIDTH_OUT)
+MIDDLE = {"p": (0.0, 4.5, 8.5, 13.0, 18.0, 22.0), "d": (0.0, 4.5, 10.5, 15.5, 23.5, 28.5, 33.0)}
+QUAD = 4
 
 
 def place():
@@ -121,8 +121,8 @@
 
 def copy_rows(move):
     def four(g, carry):
-        for j in range(4):
-            move(4 * g + j, g, j)
+        for j in range(QUAD):
+            move(g // 4, (g % 4) * 2 + j // 2, j % 2, g, j)
         return carry
 
     lax.fori_loop(0, 16, four, 0)
@@ -132,10 +132,10 @@
     cache_length, prefill_length, dtok, wkv, ptok, wq, wo, cache_hbm,
     prefill_out, decode_out,
     gp0, gp1, gda, gdb, w, wov, wt, cache, tloc, xda, xdb, dsend, drecv,
-    accp, accd, give, takep, taked, tok, s1, r2, qj, qh,
-    kvown, k2, att, heads, dec, dec2, ppa, ppb, pda, pdb, lpa, lpb, lda, ldb,
+    accp, accd, give, takep, taked, tok, tokp, backp, s1, r1, r2, qj, qjp, qh,
+    kvown, k1, k2, att, heads, dec, dec2, ppa, ppb, pda, pdb, lpa, lpb, lda, ldb,
     opa, opb, oda, odb, psend, precv, dsend2, drecv2, pfin, pland,
-    local, esend, erecv, send, recv, gsend, grecv, asend, arecv, hsend, hrecv,
+    local, esend, erecv, send, recv, gsend, grecv, asend, arecv, ksend, krecv, qsend, qrecv, hsend, hrecv,
     osend, orecv, fsend, frecv,
 ):
     gx, x, z, yl = place()
@@ -158,7 +158,12 @@
     g_peers = [((gx + s) % GX, yz) for s in range(1, GX)]
     there = 1 - y_hi
     across = [(2 * there + o, flat(x, z, 1 - yl)) for o in range(2)]
-    many = X * Z * YL
+    z_peers = [(gx, flat(x, (z + s) % Z, yl)) for s in range(1, Z)]
+    xy_peers = [(gx, flat((x + e // 2) % X, z, (yl + e) % YL)) for e in range(1, X * YL)]
+    quad_first = (yz // QUAD) * QUAD
+    place_in_quad = yz % QUAD
+    quad_peers = [(gx, quad_first + (place_in_quad + s) % QUAD) for s in range(1, QUAD)]
+    diagonal = (gx, flat(x, z + 1 - 2 * (z % 2), 1 - yl))
 
     def remote(src, dst, ssem, rsem, device):
         return pltpu.make_async_remote_copy(
@@ -174,15 +179,10 @@
         remote(dst, dst, ssem, rsem, near("x+")).wait_recv()
 
     barrier = pltpu.get_barrier_semaphore()
-    peers = g_peers + across
+    peers = z_peers + xy_peers + [diagonal] + g_peers + across
     keeper = (x, flat(gx, z, yl))
     turned = x != gx
 
-    def greet(n, carry):
-        pl.semaphore_signal(barrier, inc=1, device_id=(gx, (yz + n) % many), device_id_type=MESH)
-        return carry
-
-    lax.fori_loop(1, many, greet, 0)
     for peer in peers:
         pl.semaphore_signal(barrier, inc=1, device_id=peer, device_id_type=MESH)
 
@@ -202,7 +202,7 @@
     dsend[:72, :256] = dtok[0]
     dsend[:72, 256:] = dtok[1]
     dsend[72:, :] = jnp.zeros((8, TOK), BF16)
-    pl.semaphore_wait(barrier, many - 1 + len(peers) + turned.astype(jnp.int32))
+    pl.semaphore_wait(barrier, len(peers) + turned.astype(jnp.int32))
 
     partner = (gx, flat(x, z, 1 - yl))
     start(dsend, drecv, esend.at[2], erecv.at[2], partner)
@@ -210,15 +210,17 @@
 
         @pl.when(core == c)
         def _(c=c):
-            for o in range(2):
-                lane = pl.multiple_of((2 * there + o) * group + x * SPAN, 128)
-                remote(
-                    ptok.at[:, pl.ds(lane, SPAN)],
-                    got["p%d" % c].at[x],
-                    esend.at[o],
-                    erecv.at[c],
-                    across[o],
-                ).start()
+            for far in range(2):
+                xx = (x + 2 * far) % X
+                for o in range(2):
+                    lane = pl.multiple_of((2 * there + o) * group + xx * SPAN, 128)
+                    remote(
+                        ptok.at[:, pl.ds(lane, SPAN)],
+                        got["p%d" % c].at[xx],
+                        esend.at[4 * far + o],
+                        erecv.at[4 * far + c],
+                        across[o],
+                    ).start()
 
     w_load = load(wq, w.at[pl.ds(0, COLS)])
     mine_load = load(ptok.at[:, pl.ds(pl.multiple_of(gx * group, 128), group)], tloc.at[0])
@@ -232,8 +234,8 @@
     )
     wo_load = load(wo, wov)
     cache_load = load(cache_hbm, cache)
-    tok[...] = jnp.zeros(tok.shape, F32)
-    qj[...] = jnp.zeros(qj.shape, F32)
+    for ref in (tok, tokp, qj):
+        ref[...] = jnp.zeros(ref.shape, F32)
 
     def slot(key, rows):
         kind, xo, zo = key
@@ -270,7 +272,10 @@
     def gather_node(key):
         kind, xo, zo = key
         mine = (xo, zo) == (0, 0)
-        if not mine:
+        if xo == 2 and kind in FAR:
+            c = 4 + int(kind[1])
+            arrive(slot(key, FULL), esend.at[c], erecv.at[c])
+        elif not mine:
             for _, rows in IN.pieces[key]:
                 k = IN.fills[(key, rows)]
                 arrive(slot(key, rows), send.at[KINDS_IN.index(kind)], recv.at[k])
@@ -319,24 +324,35 @@
 
     n_of = {"p": 0, "d": 1}
 
-    def exchange_start(i, also=None):
-        def one(n, carry):
-            to = (yz + n) % many
-            remote(s1.at[i, to], r2.at[i, yz], asend.at[i], arecv.at[i], (gx, to)).start()
-            if also:
-                remote(kvown, k2.at[yz], asend.at[4], arecv.at[4], (gx, to)).start()
-            return carry
-
-        lax.fori_loop(1, many, one, 0)
-        r2[i, yz] = s1[i, yz]
-        if also:
-            k2[yz] = kvown[...]
+    def exchange_z(i):
+        for s in range(1, Z):
+            start(
+                s1.at[i, :, (z + s) % Z],
+                r1.at[i, :, z],
+                asend.at[i, s],
+                arecv.at[i, s],
+                z_peers[s - 1],
+            )
+        r1[i, :, z] = s1[i, :, z]
+
+    def exchange_xy(i):
+        for s in range(1, Z):
+            arrive(r1.at[i, :, (z + Z - s) % Z], asend.at[i, s], arecv.at[i, s])
+        for e in range(1, X * YL):
+            start(
+                r1.at[i, (x + e // 2) % X, :, (yl + e) % YL],
+                r2.at[i, x, :, yl],
+                asend.at[i, Z + e],
+                arecv.at[i, Z + e],
+                xy_peers[e - 1],
+            )
+        r2[i, x, :, yl] = r1[i, x, :, yl]
 
     def exchange_end(i):
-        arrive(r2.at[i, pl.ds(0, many - 1)], asend.at[i], arecv.at[i])
-
-    def token(f, r, t):
-        return 2 * r + t if f == "p" else t * 64 + r
+        for e in range(1, X * YL):
+            arrive(
+                r2.at[i, (x + X - e // 2) % X, :, (yl + e) % YL], asend.at[i, Z + e], arecv.at[i, Z + e]
+            )
 
     def queries_start(f):
         for s in range(1, GX):
@@ -346,43 +362,76 @@
         for s in range(1, GX):
             total = total + take[f][s - 1].astype(F32)
         total = total.astype(BF16).astype(F32)
+        if f == "p":
+            tokp[:, :ROWS1] = total.T
+            for s in range(1, QUAD):
+                to = (place_in_quad + s) % QUAD
+                start(
+                    tokp.at[pl.ds(pl.multiple_of(32 * to, 32), 32)],
+                    qjp.at[place_in_quad],
+                    qsend.at[0, s],
+                    qrecv.at[0, s],
+                    quad_peers[s - 1],
+                )
+            qjp[place_in_quad] = tokp[pl.ds(pl.multiple_of(32 * place_in_quad, 32), 32), :]
+            kvown[...] = total[COLS : COLS + KVC]
+            for s in range(1, Z):
+                start(kvown, k1.at[z], ksend.at[s], krecv.at[s], z_peers[s - 1])
+            k1[z] = kvown[...]
+            return
         tok[:, :ROWS1] = total.T
-        i = 2 * n_of[f]
-
-        def pack(r, g, j):
+
+        def pack(xx, zz, yy, g, j):
+            r = flat(xx, zz, yy)
             for t in range(2):
-                s1[i, r, pl.ds(t, 1), :] = tok[pl.ds(token(f, r, t), 1), :]
+                s1[0, xx, zz, yy, pl.ds(t, 1), :] = tok[pl.ds(t * 64 + r, 1), :]
 
         copy_rows(pack)
-        if f == "p":
-            kvown[...] = total[COLS : COLS + KVC]
-        exchange_start(i, f == "p")
+        exchange_z(0)
+
+    def queries_pass(f):
+        if f == "d":
+            exchange_xy(0)
+            return
+        for s in range(1, Z):
+            arrive(k1.at[(z + Z - s) % Z], ksend.at[s], krecv.at[s])
+        for e in range(1, X * YL):
+            start(k1, k2.at[x, :, yl], ksend.at[Z + e], krecv.at[Z + e], xy_peers[e - 1])
+        k2[x, :, yl] = k1[...]
 
     nt = (((1,), (1,)), ((), ()))
     scale = HD ** (-0.5)
 
     def attend(f):
-        i = 2 * n_of[f]
-        exchange_end(i)
-
-        def unpack(r, g, j):
-            for t in range(2):
-                qj[j, pl.ds(t * 16 + g, 1), :] = r2[i, r, pl.ds(t, 1), :]
-
-        copy_rows(unpack)
-        qh[0:32, :192] = qj[0, :, :192]
-        qh[0:32, 192:] = qj[1, :, :64]
-        qh[32:64, :128] = qj[1, :, 64:192]
-        qh[32:64, 128:] = qj[2, :, :128]
-        qh[64:96, :64] = qj[2, :, 128:192]
-        qh[64:96, 64:] = qj[3, :, :192]
+        if f == "p":
+            for s in range(1, QUAD):
+                arrive(
+                    qjp.at[(place_in_quad + QUAD - s) % QUAD], qsend.at[0, s], qrecv.at[0, s]
+                )
+            piece = qjp
+        else:
+            exchange_end(0)
+
+            def unpack(xx, zz, yy, g, j):
+                for t in range(2):
+                    qj[j, pl.ds(t * 16 + g, 1), :] = r2[0, xx, zz, yy, pl.ds(t, 1), :]
+
+            copy_rows(unpack)
+            piece = qj
+        qh[0:32, :192] = piece[0, :, :192]
+        qh[0:32, 192:] = piece[1, :, :64]
+        qh[32:64, :128] = piece[1, :, 64:192]
+        qh[32:64, 128:] = piece[2, :, :128]
+        qh[64:96, :64] = piece[2, :, 128:192]
+        qh[64:96, 64:] = piece[3, :, :192]
         q32 = qh[...]
         q = q32.astype(BF16)
         if f == "p":
-            arrive(k2.at[pl.ds(0, many - 1)], asend.at[4], arecv.at[4])
+            for e in range(1, X * YL):
+                arrive(k2.at[(x + X - e // 2) % X, :, (yl + e) % YL], ksend.at[Z + e], krecv.at[Z + e])
             kvt = k2[...].reshape(2 * HD, PLEN).astype(BF16)
             s = jnp.dot(q, kvt[:HD], preferred_element_type=F32) * scale
-            query = 2 * yz + (lax.broadcasted_iota(jnp.int32, s.shape, 0) // 16) % 2
+            query = 32 * place_in_quad + lax.broadcasted_iota(jnp.int32, s.shape, 0) % 32
             pos = lax.broadcasted_iota(jnp.int32, s.shape, 1)
             s = jnp.where((pos <= query) & (pos < prefill_length[0]), s, -1e30)
             e = jnp.exp(s - jnp.max(s, axis=1, keepdims=True))
@@ -416,31 +465,54 @@
             out = out + (e0 / total).astype(BF16).astype(F32) * new0[:, HD:]
             out = out + (e1 / total).astype(BF16).astype(F32) * new1[:, HD:]
         qh[...] = out.astype(BF16).astype(F32)
-        qj[0, :, :192] = qh[0:32, :192]
-        qj[1, :, :64] = qh[0:32, 192:]
-        qj[1, :, 64:192] = qh[32:64, :128]
-        qj[2, :, :128] = qh[32:64, 128:]
-        qj[2, :, 128:192] = qh[64:96, :64]
-        qj[3, :, :192] = qh[64:96, 64:]
-
-        def pack(r, g, j):
+        piece[0, :, :192] = qh[0:32, :192]
+        piece[1, :, :64] = qh[0:32, 192:]
+        piece[1, :, 64:192] = qh[32:64, :128]
+        piece[2, :, :128] = qh[32:64, 128:]
+        piece[2, :, 128:192] = qh[64:96, :64]
+        piece[3, :, :192] = qh[64:96, 64:]
+
+        if f == "p":
+            for s in range(1, QUAD):
+                start(
+                    piece.at[(place_in_quad + s) % QUAD],
+                    backp.at[pl.ds(pl.multiple_of(32 * place_in_quad, 32), 32)],
+                    qsend.at[1, s],
+                    qrecv.at[1, s],
+                    quad_peers[s - 1],
+                )
+            backp[pl.ds(pl.multiple_of(32 * place_in_quad, 32), 32), :] = piece[place_in_quad]
+            return
+
+        def pack(xx, zz, yy, g, j):
             for t in range(2):
-                s1[i + 1, r, pl.ds(t, 1), :] = qj[j, pl.ds(t * 16 + g, 1), :]
+                s1[1, xx, zz, yy, pl.ds(t, 1), :] = qj[j, pl.ds(t * 16 + g, 1), :]
 
         copy_rows(pack)
-        exchange_start(i + 1)
+        exchange_z(1)
+
+    def attended_pass(f):
+        exchange_xy(1)
 
     def attended_share(f):
         n = n_of[f]
-        i = 2 * n + 1
-        exchange_end(i)
-
-        def unpack(r, g, j):
-            for t in range(2):
-                tok[pl.ds(token(f, r, t), 1), :] = r2[i, r, pl.ds(t, 1), :]
-
-        copy_rows(unpack)
-        att[n] = tok[...].T[:COLS].astype(BF16)
+        if f == "p":
+            for s in range(1, QUAD):
+                first = 32 * ((place_in_quad + QUAD - s) % QUAD)
+                arrive(
+                    backp.at[pl.ds(pl.multiple_of(first, 32), 32)], qsend.at[1, s], qrecv.at[1, s]
+                )
+            att[n] = backp[...].T[:COLS].astype(BF16)
+        else:
+            exchange_end(1)
+
+            def unpack(xx, zz, yy, g, j):
+                r = flat(xx, zz, yy)
+                for t in range(2):
+                    tok[pl.ds(t * 64 + r, 1), :] = r2[1, xx, zz, yy, pl.ds(t, 1), :]
+
+            copy_rows(unpack)
+            att[n] = tok[...].T[:COLS].astype(BF16)
         for s in range(1, GX):
             start(att.at[n], heads.at[n, s], hsend.at[n, s], hrecv.at[n, s], g_peers[s - 1])
         heads[n, 0] = att[n]
@@ -544,17 +616,28 @@
         multiply_near(1)
         cache_load.wait()
 
-    middle = (sum_start, queries_start, attend, attended_share, attended_end)
+    middle = {
+        "p": (sum_start, queries_start, queries_pass, attend, attended_share, attended_end),
+        "d": (
+            sum_start,
+            queries_start,
+            queries_pass,
+            attend,
+            attended_pass,
+            attended_share,
+            attended_end,
+        ),
+    }
     todo = [(IN.times[key], gather_node, key) for key in IN.order]
     todo.append((1.5, lambda _: weights(), None))
     todo.append((9.0, lambda _: sibling(), None))
     ends = {}
     for f in "pd":
         ready = max(IN.times[key] for key in IN.order if key[0][0] == f) + 0.5
-        todo += [(ready + MIDDLE[n], step, f) for n, step in enumerate(middle)]
-        ends[f] = ready + MIDDLE[-1]
+        todo += [(ready + after, step, f) for after, step in zip(MIDDLE[f], middle[f])]
+        ends[f] = ready + MIDDLE[f][-1]
         if f == "p":
-            todo.append((ready + MIDDLE[1] + 0.1, lambda _: turn_weights(), None))
+            todo.append((ready + MIDDLE["p"][1] + 0.1, lambda _: turn_weights(), None))
     begin = ends["p"] + 0.1
     out_times = {key: begin + OUT.end - OUT.times[key] for key in OUT.order}
     first_d = min(t for key, t in out_times.items() if key[0][0] == "d")
@@ -578,19 +661,14 @@
         decode_out[t] = dec_sum[:, t * 256 : t * 256 + 256].astype(BF16)
 
     for n, kind in enumerate(KINDS_IN):
-        sent = got[kind].at[pl.ds(0, 3 if kind[0] == "p" else X * Z - 1)]
+        sent = got[kind].at[pl.ds(0, 2 if kind[0] == "p" else X * Z - 1)]
         remote(sent, sent, send.at[n], recv.at[0], partner).wait_send()
     for n, kind in enumerate(KINDS):
         sent = held[kind].at[pl.ds(0, X * Z - 1)]
         remote(sent, sent, osend.at[n], orecv.at[0], partner).wait_send()
-    for o in range(2):
+    for o in (0, 1, 4, 5):
         sent = got["p0"].at[0]
         remote(sent, sent, esend.at[o], erecv.at[o], partner).wait_send()
-    for i in range(4):
-        sent = s1.at[i, pl.ds(0, many - 1)]
-        remote(sent, sent, asend.at[i], arecv.at[i], partner).wait_send()
-    sent = k2.at[pl.ds(0, many - 1)]
-    remote(sent, sent, asend.at[4], arecv.at[4], partner).wait_send()
     for c in pending:
         c.wait_send()
 
@@ -632,12 +710,17 @@
             scratch(GX - 1, ROWS1, 128),
             scratch(GX - 1, ROWS1, 128),
             scratch(128, 256, dtype=F32),
-            scratch(4, X * Z * YL, 2, 256, dtype=F32),
-            scratch(4, X * Z * YL, 2, 256, dtype=F32),
-            scratch(4, 32, 256, dtype=F32),
+            scratch(128, 256, dtype=F32),
+            scratch(128, 256, dtype=F32),
+            scratch(2, X, Z, YL, 2, 256, dtype=F32),
+            scratch(2, X, Z, YL, 2, 256, dtype=F32),
+            scratch(2, X, Z, YL, 2, 256, dtype=F32),
+            scratch(QUAD, 32, 256, dtype=F32),
+            scratch(QUAD, 32, 256, dtype=F32),
             scratch(96, 256, dtype=F32),
             scratch(KVC, PLEN, dtype=F32),
-            scratch(X * Z * YL, KVC, PLEN, dtype=F32),
+            scratch(Z, KVC, PLEN, dtype=F32),
+            scratch(X, Z, YL, KVC, PLEN, dtype=F32),
             scratch(2, COLS, 128),
             scratch(2, GX, COLS, 128),
             scratch(COLS, TOK),
@@ -654,14 +737,18 @@
             scratch(2 * BLK, PLEN),
             scratch(2 * BLK, PLEN),
             dma((4,)),
-            dma((4,)),
-            dma((4,)),
+            dma((6,)),
+            dma((6,)),
             dma((4,)),
             dma((len(IN.sends),)),
             dma((2, GX)),
             dma((2, GX)),
-            dma((5,)),
-            dma((5,)),
+            dma((2, 16)),
+            dma((2, 16)),
+            dma((16,)),
+            dma((16,)),
+            dma((2, QUAD)),
+            dma((2, QUAD)),
             dma((2, GX)),
             dma((2, GX)),
             dma((4,)),
@@ -670,7 +757,7 @@
             dma((3,)),
         ],
         compiler_params=pltpu.CompilerParams(
-            collective_id=0, has_side_effects=True, vmem_limit_bytes=60 * 2**20
+            collective_id=0, has_side_effects=True, vmem_limit_bytes=56 * 2**20
         ),
         name="attention_block",
     )(cache_length, prefill_length, dtok, wkv, ptok, wq, wo, cache)

time: 157 us -> 152 us (0.968)
  Pallas kernels: 151 us -> 147 us
    pallas_call x1, Pallas kernels: 151 us -> 147 us  [run(): pl.pallas_call(kernel, out_shape=(jax.ShapeDtypeStruct((2 * BLK, PLEN), B...]
where the time goes in v5:
time: 152 us
  Pallas kernels  147 us (97%)
  local copies, waits for them, and re-layouts  3.04 us (2%)
  between operations  1.93 us (1%)
    pallas_call x1, Pallas kernels, run(): pl.pallas_call(kernel, out_shape=(jax.ShapeDtypeStruct((2 * BLK, PLEN), B...  147 us
    unnamed x2, local copies, waits for them, and re-layouts  3.04 us

profile of v5, /device:TPU:16, one launch (start us, length us, event | category | flops | bytes accessed | tf_op | source)
XLA Modules:
  0.0 151.6 jit_solution(8887833117773592440)
XLA Ops:
  1.9 146.7 %attention_block.1 = (bf16[288,128]{1,0:T(8,128)(2,1)}, bf16[2,72,256]{2,1,0:T(8,128)(2,1)}) custom-call(s32[1]{0:T(128)S(6)} %copy.13.cache_length, s32[1]{0:T(128)S(6)} %copy.12.prefill_length, bf16[2,72,256]{2,1,0:T(8,128)(2,1)} %bitcast.10, bf16[8,4608]{1,0:T(8,128)(2,1)} %bitcast.11, bf16[128,18432]{1,0:T(8,128)(2,1)} %ptok.1, ...), custom_call_target="tpu_custom_call" | custom-call | tf_op jit(solution)/shard_map/attention_block/pallas_call | solution.py:685
  148.6 1.5 %copy.14 = bf16[128,288]{0,1:T(8,128)(2,1)} copy(bf16[128,288]{0,1:T(8,128)(2,1)} %bitcast.9) | data formatting | bytes 147456
  150.1 1.5 %copy.15 = bf16[2,256,72]{1,2,0:T(8,128)(2,1)} copy(bf16[2,256,72]{1,2,0:T(8,128)(2,1)} %bitcast.8) | data formatting | bytes 147456

commit v6 on v5

--- a/solution.py
+++ b/solution.py
@@ -104,7 +104,7 @@
 
 
 IN = Plan({"db": 0.0, "da": 0.0, "p0": 9.0, "p1": 15.0}, WIDTH_IN)
-OUT = Plan({"db": 0.0, "da": 0.0, "pb": 20.0, "pa": 20.0}, WIDTH_OUT)
+OUT = Plan({"db": 0.0, "da": 0.0, "pb": 28.0, "pa": 28.0}, WIDTH_OUT)
 MIDDLE = {"p": (0.0, 4.5, 8.5, 13.0, 18.0, 22.0), "d": (0.0, 4.5, 10.5, 15.5, 23.5, 28.5, 33.0)}
 QUAD = 4
 

time: 152 us -> 150 us (0.987)
  Pallas kernels: 147 us -> 143 us
    pallas_call x1, Pallas kernels: 147 us -> 143 us  [run(): pl.pallas_call(kernel, out_shape=(jax.ShapeDtypeStruct((2 * BLK, PLEN), B...]
where the time goes in v6:
time: 150 us; the launch traced here: 148 us
  Pallas kernels  143 us (95%)
  local copies, waits for them, and re-layouts  3.04 us (2%)
  between operations  1.93 us (1%)
    pallas_call x1, Pallas kernels, run(): pl.pallas_call(kernel, out_shape=(jax.ShapeDtypeStruct((2 * BLK, PLEN), B...  143 us
    unnamed x2, local copies, waits for them, and re-layouts  3.04 us

profile of v6, /device:TPU:16, one launch (start us, length us, event | category | flops | bytes accessed | tf_op | source)
XLA Modules:
  0.0 148.2 jit_solution(13995756524293062962)
XLA Ops:
  1.9 143.2 %attention_block.1 = (bf16[288,128]{1,0:T(8,128)(2,1)}, bf16[2,72,256]{2,1,0:T(8,128)(2,1)}) custom-call(s32[1]{0:T(128)S(6)} %copy.13.cache_length, s32[1]{0:T(128)S(6)} %copy.12.prefill_length, bf16[2,72,256]{2,1,0:T(8,128)(2,1)} %bitcast.10, bf16[8,4608]{1,0:T(8,128)(2,1)} %bitcast.11, bf16[128,18432]{1,0:T(8,128)(2,1)} %ptok.1, ...), custom_call_target="tpu_custom_call" | custom-call | tf_op jit(solution)/shard_map/attention_block/pallas_call | solution.py:685
  145.1 1.5 %copy.14 = bf16[128,288]{0,1:T(8,128)(2,1)} copy(bf16[128,288]{0,1:T(8,128)(2,1)} %bitcast.9) | data formatting | bytes 147456
  146.7 1.5 %copy.15 = bf16[2,256,72]{1,2,0:T(8,128)(2,1)} copy(bf16[2,256,72]{1,2,0:T(8,128)(2,1)} %bitcast.8) | data formatting | bytes 147456

commit v7 on v6

--- a/solution.py
+++ b/solution.py
@@ -104,7 +104,7 @@
 
 
 IN = Plan({"db": 0.0, "da": 0.0, "p0": 9.0, "p1": 15.0}, WIDTH_IN)
-OUT = Plan({"db": 0.0, "da": 0.0, "pb": 28.0, "pa": 28.0}, WIDTH_OUT)
+OUT = Plan({"db": 0.0, "da": 0.0, "pb": 25.0, "pa": 25.0}, WIDTH_OUT)
 MIDDLE = {"p": (0.0, 4.5, 8.5, 13.0, 18.0, 22.0), "d": (0.0, 4.5, 10.5, 15.5, 23.5, 28.5, 33.0)}
 QUAD = 4
 

time: 150 us -> 151 us (level)
  Pallas kernels: 143 us -> 145 us
    pallas_call x1, Pallas kernels: 143 us -> 145 us  [run(): pl.pallas_call(kernel, out_shape=(jax.ShapeDtypeStruct((2 * BLK, PLEN), B...]
where the time goes in v7:
time: 151 us; the launch traced here: 150 us
  Pallas kernels  145 us (96%)
  local copies, waits for them, and re-layouts  3.04 us (2%)
  between operations  1.93 us (1%)
    pallas_call x1, Pallas kernels, run(): pl.pallas_call(kernel, out_shape=(jax.ShapeDtypeStruct((2 * BLK, PLEN), B...  145 us
    unnamed x2, local copies, waits for them, and re-layouts  3.04 us

profile of v7, /device:TPU:16, one launch (start us, length us, event | category | flops | bytes accessed | tf_op | source)
XLA Modules:
  0.0 150.4 jit_solution(2260064801857249649)
XLA Ops:
  1.9 145.4 %attention_block.1 = (bf16[288,128]{1,0:T(8,128)(2,1)}, bf16[2,72,256]{2,1,0:T(8,128)(2,1)}) custom-call(s32[1]{0:T(128)S(6)} %copy.13.cache_length, s32[1]{0:T(128)S(6)} %copy.12.prefill_length, bf16[2,72,256]{2,1,0:T(8,128)(2,1)} %bitcast.10, bf16[8,4608]{1,0:T(8,128)(2,1)} %bitcast.11, bf16[128,18432]{1,0:T(8,128)(2,1)} %ptok.1, ...), custom_call_target="tpu_custom_call" | custom-call | tf_op jit(solution)/shard_map/attention_block/pallas_call | solution.py:685
  147.3 1.5 %copy.14 = bf16[128,288]{0,1:T(8,128)(2,1)} copy(bf16[128,288]{0,1:T(8,128)(2,1)} %bitcast.9) | data formatting | bytes 147456
  148.8 1.5 %copy.15 = bf16[2,256,72]{1,2,0:T(8,128)(2,1)} copy(bf16[2,256,72]{1,2,0:T(8,128)(2,1)} %bitcast.8) | data formatting | bytes 147456
